TPU v7x, 32 devices: a whole 2x2x4 slice. The times are simulated.
32 devices in a mesh: depth: 4 (over y, x), lat: 8 (over z, core).
Axes of the slice: x: 2, y: 2, z: 4, core: 2. Of those that a mesh axis runs over, the one named last changes fastest.
Arguments:
- probe: float32 [2, 256, 256], replicated, may hold values from -4 to 4
- prop_phase: float32 [256, 256], replicated, may hold values from -3.140625 to 3.140625
- object_field: float32 [2, 8, 2048, 1024], P(None, 'depth', 'lat'), may hold values from -1.2 to 2.1, as said below
- measured: float32 [16, 256, 256], P('lat'), may hold values from 0 to 2
- offsets: int32 [16, 2], P('lat'), may hold values from 0 to 1792, as said below
Outputs:
- object_gradient: float32 [2, 8, 2048, 1024], P(None, 'depth', 'lat')
Inputs may be any that keep to these rules, and one draw needn't show every extreme that they name: object_field holds each slice's complex transmission, real part first. `offsets`: row j holds the first row and first column of position j's 256 x 256 patch, which lies inside the object; the first row lies in row tile j // 2 or in the tile before it, tile k being rows k * 256 to (k + 1) * 256 - 1.
All inputs are finite; a program needn't handle non-finite values.
Results may differ from a plain program's by a relative error of at most 0.0003.
Values sent between devices are 32-bit elements; how exact they have to be, the bound alone decides.
A program may use at most 128 MiB of HBM per device.

v0:
```python
import math

import jax
import jax.numpy as jnp
from jax import lax
from jax.sharding import PartitionSpec as P


def with_halo(x, sides, width):
    for axis, dim in sides:
        peers, length = (lax.axis_size(axis), x.shape[dim])
        up = [(i, (i + 1) % peers) for i in range(peers - 1)]
        down = [(j, i) for i, j in up]
        last = lax.slice_in_dim(x, length - width, length, axis=dim)
        initial = lax.slice_in_dim(x, 0, width, axis=dim)
        before = lax.ppermute(last, axis, up)
        after = lax.ppermute(initial, axis, down)
        x = jnp.concatenate([before, x, after], axis=dim)
    return x


def passed_along(value, axis, steps):
    count = lax.axis_size(axis)
    initial, last = (max(0, -steps), min(count, count - steps))
    return lax.ppermute(value, axis, [(source, source + steps) for source in range(initial, last)])


def dft_tables(length):
    counter = jnp.arange(length, dtype=jnp.int32)
    phase = counter[:, None] * counter[None, :] % length
    angle = phase.astype(jnp.float32) * (2.0 * math.pi / length)
    factor = 1.0 / math.sqrt(length)
    return (jnp.cos(angle) * factor, jnp.sin(angle) * factor)


def matmul_exact(left, right):
    return jnp.matmul(left, right, precision=lax.Precision.HIGHEST)


def transform(values, cosine, sine, direction):
    re_part = values[..., 0, :, :]
    im_part = values[..., 1, :, :]
    left_re = matmul_exact(cosine, re_part) - direction * matmul_exact(sine, im_part)
    left_im = matmul_exact(cosine, im_part) + direction * matmul_exact(sine, re_part)
    out_re = matmul_exact(left_re, cosine) - direction * matmul_exact(left_im, sine)
    out_im = matmul_exact(left_im, cosine) + direction * matmul_exact(left_re, sine)
    return jnp.stack([out_re, out_im], axis=-3)


def complex_product(first, second):
    first_re = first[..., 0, :, :]
    first_im = first[..., 1, :, :]
    second_re = second[..., 0, :, :]
    second_im = second[..., 1, :, :]
    return jnp.stack(
        [first_re * second_re - first_im * second_im, first_re * second_im + first_im * second_re],
        axis=-3,
    )


def conj_product(first, second):
    first_re = first[..., 0, :, :]
    first_im = first[..., 1, :, :]
    second_re = second[..., 0, :, :]
    second_im = second[..., 1, :, :]
    return jnp.stack(
        [first_re * second_re + first_im * second_im, first_re * second_im - first_im * second_re],
        axis=-3,
    )


def propagate(values, kernel, cosine, sine, adjoint):
    spectrum = transform(values, cosine, sine, -1.0)
    if adjoint:
        spectrum = conj_product(kernel, spectrum)
    else:
        spectrum = complex_product(kernel, spectrum)
    return transform(spectrum, cosine, sine, 1.0)


def local(probe, prop_phase, object_field, measured, offsets):
    width = probe.shape[-1]
    cosine, sine = dft_tables(width)
    kernel = jnp.stack([jnp.cos(prop_phase), jnp.sin(prop_phase)], axis=0)
    slab_depth = object_field.shape[1]
    tile_rows = object_field.shape[2]
    owned_count = offsets.shape[0]
    depth_count = lax.axis_size("depth")
    depth_rank = lax.axis_index("depth")
    lateral_rank = lax.axis_index("lat")
    first_section = depth_rank == 0
    last_section = depth_rank == depth_count - 1
    zero_index = jnp.zeros((), jnp.int32)
    row_starts = offsets[:, 0] - (lateral_rank - 1) * tile_rows
    col_starts = offsets[:, 1]
    region = with_halo(object_field, (("lat", 2),), tile_rows)

    def cut_window(row_start, col_start):
        return lax.dynamic_slice(
            region, (zero_index, zero_index, row_start, col_start), (2, slab_depth, width, width)
        )

    windows = jax.vmap(cut_window)(row_starts, col_starts)
    windows = jnp.transpose(windows, (0, 2, 1, 3, 4))

    def forward_slab(entering, window):
        stored = []
        wavefield = entering
        for layer_index in range(slab_depth):
            stored.append(wavefield)
            exiting = complex_product(window[:, layer_index], wavefield)
            if layer_index + 1 < slab_depth:
                wavefield = propagate(exiting, kernel, cosine, sine, False)
            else:
                wavefield = lax.cond(
                    last_section,
                    lambda held: held,
                    lambda held: propagate(held, kernel, cosine, sine, False),
                    exiting,
                )
        return (wavefield, jnp.stack(stored, axis=1))

    def far_field(exiting, targets):
        farfield = transform(exiting, cosine, sine, -1.0)
        intensity = farfield[:, 0] * farfield[:, 0] + farfield[:, 1] * farfield[:, 1]
        misfit = intensity - targets
        return transform(misfit[:, None] * farfield, cosine, sine, 1.0)

    def backward_slab(adjoint, window, stored):
        terms = [None] * slab_depth
        for layer_index in reversed(range(slab_depth)):
            terms[layer_index] = conj_product(stored[:, layer_index], adjoint)
            moved = conj_product(window[:, layer_index], adjoint)
            if layer_index > 0:
                adjoint = propagate(moved, kernel, cosine, sine, True)
            else:
                adjoint = lax.cond(
                    first_section,
                    lambda held: held,
                    lambda held: propagate(held, kernel, cosine, sine, True),
                    moved,
                )
        return (adjoint, jnp.stack(terms, axis=1))

    block_size = 1
    batch_count = owned_count // block_size
    step_count = batch_count + depth_count - 1
    shape_block = (block_size, 2, width, width)
    source = jnp.broadcast_to(probe, shape_block)

    def forward_turn(turn, carry):
        inflow, saved, starts = carry
        micro_batch = turn - depth_rank
        active = (micro_batch >= 0) & (micro_batch < batch_count)
        first_row = jnp.clip(micro_batch, 0, batch_count - 1) * block_size
        window = lax.dynamic_slice_in_dim(windows, first_row, block_size, 0)
        targets = lax.dynamic_slice_in_dim(measured, first_row, block_size, 0)
        previous_saved = lax.dynamic_slice_in_dim(saved, first_row, block_size, 0)
        previous_start = lax.dynamic_slice_in_dim(starts, first_row, block_size, 0)
        entering = jnp.where(first_section, source, inflow)

        def forward_working(operands):
            wave_in, window_in, target_in, saved_in, start_in = operands
            leaving, stored = forward_slab(wave_in, window_in)
            begin = lax.cond(
                last_section,
                lambda held: far_field(held[0], held[1]),
                lambda held: held[2],
                (leaving, target_in, start_in),
            )
            return (leaving, stored, begin)

        def forward_waiting(operands):
            wave_in, window_in, target_in, saved_in, start_in = operands
            return (jnp.zeros(shape_block, jnp.float32), saved_in, start_in)

        leaving, stored, begin = lax.cond(
            active,
            forward_working,
            forward_waiting,
            (entering, window, targets, previous_saved, previous_start),
        )
        saved = lax.dynamic_update_slice_in_dim(saved, stored, first_row, 0)
        starts = lax.dynamic_update_slice_in_dim(starts, begin, first_row, 0)
        outflow = passed_along(leaving, "depth", 1)
        return (outflow, saved, starts)

    initial_saved = jnp.zeros((owned_count, slab_depth, 2, width, width), jnp.float32)
    initial_starts = jnp.zeros((owned_count, 2, width, width), jnp.float32)
    unused_flow, saved, starts = lax.fori_loop(
        0,
        step_count,
        forward_turn,
        (jnp.zeros(shape_block, jnp.float32), initial_saved, initial_starts),
    )

    def backward_turn(turn, carry):
        inflow, gradients = carry
        micro_batch = turn - (depth_count - 1 - depth_rank)
        active = (micro_batch >= 0) & (micro_batch < batch_count)
        first_row = jnp.clip(micro_batch, 0, batch_count - 1) * block_size
        window = lax.dynamic_slice_in_dim(windows, first_row, block_size, 0)
        stored = lax.dynamic_slice_in_dim(saved, first_row, block_size, 0)
        begin = lax.dynamic_slice_in_dim(starts, first_row, block_size, 0)
        previous_terms = lax.dynamic_slice_in_dim(gradients, first_row, block_size, 0)
        entering = jnp.where(last_section, begin, inflow)

        def backward_working(operands):
            wave_in, window_in, stored_in, terms_in = operands
            return backward_slab(wave_in, window_in, stored_in)

        def backward_waiting(operands):
            wave_in, window_in, stored_in, terms_in = operands
            return (jnp.zeros(shape_block, jnp.float32), terms_in)

        leaving, terms = lax.cond(
            active, backward_working, backward_waiting, (entering, window, stored, previous_terms)
        )
        gradients = lax.dynamic_update_slice_in_dim(gradients, terms, first_row, 0)
        outflow = passed_along(leaving, "depth", -1)
        return (outflow, gradients)

    unused_back, gradients = lax.fori_loop(
        0, step_count, backward_turn, (jnp.zeros(shape_block, jnp.float32), initial_saved)
    )
    placed = jnp.transpose(gradients, (0, 2, 1, 3, 4))

    def deposit(position, total):
        start = (zero_index, zero_index, row_starts[position], col_starts[position])
        current = lax.dynamic_slice(total, start, (2, slab_depth, width, width))
        return lax.dynamic_update_slice(total, current + placed[position], start)

    total = lax.fori_loop(0, owned_count, deposit, jnp.zeros(region.shape, jnp.float32))
    upper_rows = total[:, :, :tile_rows]
    lower_rows = total[:, :, 2 * tile_rows :]
    from_below = passed_along(upper_rows, "lat", -1)
    from_above = passed_along(lower_rows, "lat", 1)
    return total[:, :, tile_rows : 2 * tile_rows] + from_below + from_above


def solution(mesh):
    in_specs = (P(), P(), P(None, "depth", "lat", None), P("lat", None, None), P("lat", None))
    out_specs = P(None, "depth", "lat", None)
    return jax.shard_map(local, mesh=mesh, in_specs=in_specs, out_specs=out_specs, check_vma=False)
```

profile of v0, /device:TPU:1, one launch (start us, length us, event | category | flops | bytes accessed | tf_op | source)
XLA Modules:
  0.0 573.8 jit_solution(3371685700630376186)
XLA Ops:
  0.0 4.6 collective-permute-start.2
  10.0 40.3 %collective-permute-done.2 = f32[2,2,256,1024]{3,2,1,0:T(8,128)} collective-permute-done((f32[2,2,256,1024]{3,2,1,0:T(8,128)}, f32[2,2,256,1024]{3,2,1,0:T(8,128)}, u32[]{:S(2)}, u32[]{:S(2)}) %collective-permute-start.2) | collective-permute-done | bytes 4194336 | tf_op jit(solution)/shard_map/ppermute | solution.py:16
  54.7 9.6 %pad_maximum_fusion.7 = f32[2,2,768,1024]{3,2,1,0:T(8,128)} fusion(f32[2,2,256,1024]{3,2,1,0:T(8,128)} %collective-permute-done.3, f32[2,2,256,1024]{3,2,1,0:T(8,128)} %param.23, f32[2,2,256,1024]{3,2,1,0:T(8,128)} %collective-permute-done.2), kind=kLoop, calls=%fused_computation.205 | loop fusion | flops 6291456 | bytes 25165824 | tf_op jit(solution)/shard_map/concatenate | solution.py:18
  64.3 9.6 %while.53 = (s32[]{:T(128)}, f32[2,2,768,1024]{3,2,1,0:T(8,128)}, s32[2,4]{1,0:T(2,128)S(1)}, f32[2,2,2,256,256]{4,3,1,2,0:T(8,128)}, s32[]{:T(128)}) while((s32[]{:T(128)}, f32[2,2,768,1024]{3,2,1,0:T(8,128)}, s32[2,4]{1,0:T(2,128)S(1)}, f32[2,2,2,256,256]{4,3,1,2,0:T(8,128)}, s32[]{:T(128)}) %tuple.298), condition=%wide.while_cond, body=%wide.while_body.sunk | while | flops 2 | bytes 2098801 | solution.py:99
  76.5 167.0 %while.54 = (s32[]{:T(128)}, f32[1,2,256,256]{3,2,1,0:T(8,128)S(1)}, f32[2,2,2,256,256]{4,3,2,1,0:T(8,128)}, f32[2,2,256,256]{3,2,1,0:T(8,128)}, s32[]{:T(128)},...) while((s32[]{:T(128)}, ...), condition=%wide.region_7.8_spmd.clone.clone, body=%wide.region_0.7_spmd.clone.clone.sunk | while | flops 9670098944 | bytes 71829280 | solution.py:190
  77.8 23.8 %conditional.14 = (f32[1,2,256,256]{3,2,1,0:T(8,128)}, f32[1,2,2,256,256]{4,3,2,1,0:T(8,128)S(1)}, f32[1,2,256,256]{3,2,1,0:T(8,128)S(1)}) conditional(s32[]{:T(128)} %convert_element_type.222, (f32[2,2,2,256,256]{4,3,2,1,0:T(8,128)}, s32[]{:T(128)}, f32[1,2,256,256]{3,2,1,0:T(8,128)S(1)}) %tuple.289, (pred[]{:T(512)}, ...), branch_computations={%region_1.1_spmd, %region_2.6_spmd.clone} | conditional | flops 9669181440 | bytes 65012120 | solution.py:177
  92.6 8.8 %conditional.9 = (f32[1,2,256,256]{3,2,1,0:T(8,128)}) conditional(s32[]{:T(128)} %convert_element_type.209, (f32[256,256]{1,0:T(8,128)S(1)}, f32[256,256]{1,0:T(8,128)S(1)}, f32[256,256]{1,0:T(8,128)S(1)}, f32[256,256]{1,0:T(8,128)S(1)}, f32[256,256]{1,0:T(8,128)S(1)}, /*index=5*/f32[256,256]{1,0:T(8,128)S(1)}, f32[256,256]{1,0:T(8,128)S(1)}, ...), branch_computations={%region_3.2_spmd, %region_4.3_spmd} | conditional | flops 3222536192 | bytes 16777224 | solution.py:115
  104.8 4.8 collective-permute-done
  110.9 23.8 %conditional.14 = (f32[1,2,256,256]{3,2,1,0:T(8,128)}, f32[1,2,2,256,256]{4,3,2,1,0:T(8,128)S(1)}, f32[1,2,256,256]{3,2,1,0:T(8,128)S(1)}) conditional(s32[]{:T(128)} %convert_element_type.222, (f32[2,2,2,256,256]{4,3,2,1,0:T(8,128)}, s32[]{:T(128)}, f32[1,2,256,256]{3,2,1,0:T(8,128)S(1)}) %tuple.289, (pred[]{:T(512)}, ...), branch_computations={%region_1.1_spmd, %region_2.6_spmd.clone} | conditional | flops 9669181440 | bytes 65012120 | solution.py:177
  125.7 8.8 %conditional.9 = (f32[1,2,256,256]{3,2,1,0:T(8,128)}) conditional(s32[]{:T(128)} %convert_element_type.209, (f32[256,256]{1,0:T(8,128)S(1)}, f32[256,256]{1,0:T(8,128)S(1)}, f32[256,256]{1,0:T(8,128)S(1)}, f32[256,256]{1,0:T(8,128)S(1)}, f32[256,256]{1,0:T(8,128)S(1)}, /*index=5*/f32[256,256]{1,0:T(8,128)S(1)}, f32[256,256]{1,0:T(8,128)S(1)}, ...), branch_computations={%region_3.2_spmd, %region_4.3_spmd} | conditional | flops 3222536192 | bytes 16777224 | solution.py:115
  139.3 6.0 %collective-permute-done = f32[1,2,256,256]{3,2,1,0:T(8,128)S(1)} collective-permute-done((f32[1,2,256,256]{3,2,1,0:T(8,128)}, f32[1,2,256,256]{3,2,1,0:T(8,128)S(1)}, u32[]{:S(2)}, u32[]{:S(2)}) %collective-permute-start) | collective-permute-done | bytes 524320 | tf_op jit(solution)/shard_map/while/body/eval_jaxpr/ppermute | solution.py:25
  148.6 24.3 %collective-permute-start = (f32[1,2,256,256]{3,2,1,0:T(8,128)}, f32[1,2,256,256]{3,2,1,0:T(8,128)S(1)}, u32[]{:S(2)}, u32[]{:S(2)}) collective-permute-start(f32[1,2,256,256]{3,2,1,0:T(8,128)} %get-tuple-element.1993), channel_id=1, source_target_pairs={{0,8},{8,16},{16,24},{1,9},{9,17},{17,25},{2,10},{10,18},{18,26},{... | collective-permute-start | bytes 1572872 | tf_op jit(solution)/shard_map/while/body/eval_jaxpr/ppermute | solution.py:25
  174.8 4.5 collective-permute-done
  182.8 6.0 %collective-permute-start = (f32[1,2,256,256]{3,2,1,0:T(8,128)}, f32[1,2,256,256]{3,2,1,0:T(8,128)S(1)}, u32[]{:S(2)}, u32[]{:S(2)}) collective-permute-start(f32[1,2,256,256]{3,2,1,0:T(8,128)} %get-tuple-element.1993), channel_id=1, source_target_pairs={{0,8},{8,16},{16,24},{1,9},{9,17},{17,25},{2,10},{10,18},{18,26},{... | collective-permute-start | bytes 1572872 | tf_op jit(solution)/shard_map/while/body/eval_jaxpr/ppermute | solution.py:25
  190.7 8.2 %collective-permute-done = f32[1,2,256,256]{3,2,1,0:T(8,128)S(1)} collective-permute-done((f32[1,2,256,256]{3,2,1,0:T(8,128)}, f32[1,2,256,256]{3,2,1,0:T(8,128)S(1)}, u32[]{:S(2)}, u32[]{:S(2)}) %collective-permute-start) | collective-permute-done | bytes 524320 | tf_op jit(solution)/shard_map/while/body/eval_jaxpr/ppermute | solution.py:25
  202.3 21.6 %collective-permute-start = (f32[1,2,256,256]{3,2,1,0:T(8,128)}, f32[1,2,256,256]{3,2,1,0:T(8,128)S(1)}, u32[]{:S(2)}, u32[]{:S(2)}) collective-permute-start(f32[1,2,256,256]{3,2,1,0:T(8,128)} %get-tuple-element.1993), channel_id=1, source_target_pairs={{0,8},{8,16},{16,24},{1,9},{9,17},{17,25},{2,10},{10,18},{18,26},{... | collective-permute-start | bytes 1572872 | tf_op jit(solution)/shard_map/while/body/eval_jaxpr/ppermute | solution.py:25
  225.7 4.5 collective-permute-done
  245.1 207.3 %while.55 = (s32[]{:T(128)}, f32[1,2,256,256]{3,2,1,0:T(8,128)S(1)}, f32[2,2,2,256,256]{4,3,2,1,0:T(8,128)}, s32[]{:T(128)}, pred[]{:T(512)}, /*index=5*/f32[2,2...) while((s32[]{:T(128)}, ...), condition=%wide.region_13.14_spmd.clone.clone, body=%wide.region_8.13_spmd.clone.clone.sunk | while | flops 6448349184 | bytes 54527048 | solution.py:223
  249.8 18.0 %collective-permute-done.1 = f32[1,2,256,256]{3,2,1,0:T(8,128)S(1)} collective-permute-done((f32[1,2,256,256]{3,2,1,0:T(8,128)}, f32[1,2,256,256]{3,2,1,0:T(8,128)S(1)}, u32[]{:S(2)}, u32[]{:S(2)}) %collective-permute-start.1) | collective-permute-done | bytes 524320 | tf_op jit(solution)/shard_map/while/body/eval_jaxpr/ppermute | solution.py:25
  272.4 27.0 %collective-permute-done.1 = f32[1,2,256,256]{3,2,1,0:T(8,128)S(1)} collective-permute-done((f32[1,2,256,256]{3,2,1,0:T(8,128)}, f32[1,2,256,256]{3,2,1,0:T(8,128)S(1)}, u32[]{:S(2)}, u32[]{:S(2)}) %collective-permute-start.1) | collective-permute-done | bytes 524320 | tf_op jit(solution)/shard_map/while/body/eval_jaxpr/ppermute | solution.py:25
  304.1 86.6 %collective-permute-done.1 = f32[1,2,256,256]{3,2,1,0:T(8,128)S(1)} collective-permute-done((f32[1,2,256,256]{3,2,1,0:T(8,128)}, f32[1,2,256,256]{3,2,1,0:T(8,128)S(1)}, u32[]{:S(2)}, u32[]{:S(2)}) %collective-permute-start.1) | collective-permute-done | bytes 524320 | tf_op jit(solution)/shard_map/while/body/eval_jaxpr/ppermute | solution.py:25
  390.9 15.4 %conditional.15 = (f32[1,2,256,256]{3,2,1,0:T(8,128)}, f32[1,2,2,256,256]{4,3,2,1,0:T(8,128)S(1)}) conditional(s32[]{:T(128)} %convert_element_type.224, (f32[2,2,2,256,256]{4,3,2,1,0:T(8,128)}, s32[]{:T(128)}) %tuple.292, (pred[]{:T(512)}, f32[2,2,2,256,256]{4,3,2,1,0:T(8,128)}, s32[]{:T(128)}, pred[]{:T(512)}, f32[2,2,256,256]{3,2,1,0:T(8,128)}, ...), branch_computations={%region_9.9_spmd, %region_10.12_spmd.clone} | conditional | flops 6447431680 | bytes 49807576 | solution.py:216
  408.7 17.8 %collective-permute-done.1 = f32[1,2,256,256]{3,2,1,0:T(8,128)S(1)} collective-permute-done((f32[1,2,256,256]{3,2,1,0:T(8,128)}, f32[1,2,256,256]{3,2,1,0:T(8,128)S(1)}, u32[]{:S(2)}, u32[]{:S(2)}) %collective-permute-start.1) | collective-permute-done | bytes 524320 | tf_op jit(solution)/shard_map/while/body/eval_jaxpr/ppermute | solution.py:25
  426.6 15.4 %conditional.15 = (f32[1,2,256,256]{3,2,1,0:T(8,128)}, f32[1,2,2,256,256]{4,3,2,1,0:T(8,128)S(1)}) conditional(s32[]{:T(128)} %convert_element_type.224, (f32[2,2,2,256,256]{4,3,2,1,0:T(8,128)}, s32[]{:T(128)}) %tuple.292, (pred[]{:T(512)}, f32[2,2,2,256,256]{4,3,2,1,0:T(8,128)}, s32[]{:T(128)}, pred[]{:T(512)}, f32[2,2,256,256]{3,2,1,0:T(8,128)}, ...), branch_computations={%region_9.9_spmd, %region_10.12_spmd.clone} | conditional | flops 6447431680 | bytes 49807576 | solution.py:216
  444.4 7.8 %collective-permute-done.1 = f32[1,2,256,256]{3,2,1,0:T(8,128)S(1)} collective-permute-done((f32[1,2,256,256]{3,2,1,0:T(8,128)}, f32[1,2,256,256]{3,2,1,0:T(8,128)S(1)}, u32[]{:S(2)}, u32[]{:S(2)}) %collective-permute-start.1) | collective-permute-done | bytes 524320 | tf_op jit(solution)/shard_map/while/body/eval_jaxpr/ppermute | solution.py:25
  452.4 6.1 %broadcast_in_dim.8 = f32[2,2,768,1024]{3,2,1,0:T(8,128)} broadcast(f32[]{:T(128)} %constant.175.clone.1), dimensions={} | broadcast | bytes 12582916 | tf_op jit(solution)/shard_map/broadcast_in_dim | solution.py:233
  458.5 39.3 %while.52 = (s32[]{:T(128)}, f32[2,2,768,1024]{3,2,1,0:T(8,128)}, s32[2]{0:T(128)S(1)}, s32[2]{0:T(128)S(1)}, f32[2,2,2,256,256]{4,3,1,2,0:T(8,128)}, /*index=5*/s32[]{:T(128)}, s32[]{:T(128)}, s32[]{:T(128)}, s32[]{:T(128)}) while((s32[]{:T(128)}, f32[2,2,768,1024]{3,2,1,0:T(8,128)}, s32[2]{0:T(128)S(1)}, s32[2]{0:T(128)S(1)}, ...), condition=%wide.region_15.16_spmd, body=%wide.region_14.15_spmd.sunk | while | flops 262152 | bytes 5243589 | solution.py:233
  466.1 12.3 %dynamic_update_slice.43 = f32[2,2,768,1024]{3,2,1,0:T(8,128)} dynamic-update-slice(f32[2,2,768,1024]{3,2,1,0:T(8,128)} %get-tuple-element.2137, f32[2,2,256,256]{3,2,1,0:T(8,128)S(1)} %fusion.263, s32[]{:T(128)} %constant.174.clone.1..sunk, s32[]{:T(128)} %constant.174.clone.1..sunk, s32[]{:T(128)S(6)} %select_n.298, s32[]{:T(128)S(6)} %select_n.299) | dynamic-update-slice | bytes 2097156 | tf_op jit(solution)/shard_map/while/body/eval_jaxpr/dynamic_update_slice | solution.py:231
  485.9 11.9 %dynamic_update_slice.43 = f32[2,2,768,1024]{3,2,1,0:T(8,128)} dynamic-update-slice(f32[2,2,768,1024]{3,2,1,0:T(8,128)} %get-tuple-element.2137, f32[2,2,256,256]{3,2,1,0:T(8,128)S(1)} %fusion.263, s32[]{:T(128)} %constant.174.clone.1..sunk, s32[]{:T(128)} %constant.174.clone.1..sunk, s32[]{:T(128)S(6)} %select_n.298, s32[]{:T(128)S(6)} %select_n.299) | dynamic-update-slice | bytes 2097156 | tf_op jit(solution)/shard_map/while/body/eval_jaxpr/dynamic_update_slice | solution.py:231
  504.1 18.2 %collective-permute-start.5 = (f32[2,2,256,1024]{3,2,1,0:T(8,128)S(1)}, f32[2,2,256,1024]{3,2,1,0:T(8,128)S(1)}, u32[]{:S(2)}, u32[]{:S(2)}) collective-permute-start(f32[2,2,256,1024]{3,2,1,0:T(8,128)S(1)} %get-tuple-element.1792), channel_id=1, source_target_pairs={{0,1},{1,2},{2,3},{3,4},{4,5},{5,6},{6,7},{8,9},{9,10},{10,11},{11... | collective-permute-start | bytes 12582920 | tf_op jit(solution)/shard_map/ppermute | solution.py:25
  522.4 44.2 %collective-permute-done.4 = f32[2,2,256,1024]{3,2,1,0:T(8,128)S(1)} collective-permute-done((f32[2,2,256,1024]{3,2,1,0:T(8,128)S(1)}, f32[2,2,256,1024]{3,2,1,0:T(8,128)S(1)}, u32[]{:S(2)}, u32[]{:S(2)}) %collective-permute-start.4) | collective-permute-done | bytes 4194336 | tf_op jit(solution)/shard_map/ppermute | solution.py:25
  567.8 5.7 add_add_fusion
  (229 shorter events, 172.7 us)
Async XLA Ops:
  0.0 50.3 %collective-permute-start.2 = (f32[2,2,256,1024]{3,2,1,0:T(8,128)}, f32[2,2,256,1024]{3,2,1,0:T(8,128)}, u32[]{:S(2)}, u32[]{:S(2)}) collective-permute-start(f32[2,2,256,1024]{3,2,1,0:T(8,128)} %param.23), channel_id=1, source_target_pairs={{0,1},{1,2},{2,3},{3,4},{4,5},{5,6},{6,7},{8,9},{9,10},{10,11},{11... | collective-permute-start | bytes 12582920 | tf_op jit(solution)/shard_map/ppermute | solution.py:16
  4.6 50.1 %collective-permute-start.3 = (f32[2,2,256,1024]{3,2,1,0:T(8,128)}, f32[2,2,256,1024]{3,2,1,0:T(8,128)}, u32[]{:S(2)}, u32[]{:S(2)}) collective-permute-start(f32[2,2,256,1024]{3,2,1,0:T(8,128)} %param.23), channel_id=1, source_target_pairs={{1,0},{2,1},{3,2},{4,3},{5,4},{6,5},{7,6},{9,8},{10,9},{11,10},{12... | collective-permute-start | bytes 12582920 | tf_op jit(solution)/shard_map/ppermute | solution.py:17
  101.6 8.1 %collective-permute-start = (f32[1,2,256,256]{3,2,1,0:T(8,128)}, f32[1,2,256,256]{3,2,1,0:T(8,128)S(1)}, u32[]{:S(2)}, u32[]{:S(2)}) collective-permute-start(f32[1,2,256,256]{3,2,1,0:T(8,128)} %get-tuple-element.1993), channel_id=1, source_target_pairs={{0,8},{8,16},{16,24},{1,9},{9,17},{17,25},{2,10},{10,18},{18,26},{... | collective-permute-start | bytes 1572872 | tf_op jit(solution)/shard_map/while/body/eval_jaxpr/ppermute | solution.py:25
  134.7 10.5 %collective-permute-start = (f32[1,2,256,256]{3,2,1,0:T(8,128)}, f32[1,2,256,256]{3,2,1,0:T(8,128)S(1)}, u32[]{:S(2)}, u32[]{:S(2)}) collective-permute-start(f32[1,2,256,256]{3,2,1,0:T(8,128)} %get-tuple-element.1993), channel_id=1, source_target_pairs={{0,8},{8,16},{16,24},{1,9},{9,17},{17,25},{2,10},{10,18},{18,26},{... | collective-permute-start | bytes 1572872 | tf_op jit(solution)/shard_map/while/body/eval_jaxpr/ppermute | solution.py:25
  148.6 30.7 %collective-permute-start = (f32[1,2,256,256]{3,2,1,0:T(8,128)}, f32[1,2,256,256]{3,2,1,0:T(8,128)S(1)}, u32[]{:S(2)}, u32[]{:S(2)}) collective-permute-start(f32[1,2,256,256]{3,2,1,0:T(8,128)} %get-tuple-element.1993), channel_id=1, source_target_pairs={{0,8},{8,16},{16,24},{1,9},{9,17},{17,25},{2,10},{10,18},{18,26},{... | collective-permute-start | bytes 1572872 | tf_op jit(solution)/shard_map/while/body/eval_jaxpr/ppermute | solution.py:25
  182.8 16.1 %collective-permute-start = (f32[1,2,256,256]{3,2,1,0:T(8,128)}, f32[1,2,256,256]{3,2,1,0:T(8,128)S(1)}, u32[]{:S(2)}, u32[]{:S(2)}) collective-permute-start(f32[1,2,256,256]{3,2,1,0:T(8,128)} %get-tuple-element.1993), channel_id=1, source_target_pairs={{0,8},{8,16},{16,24},{1,9},{9,17},{17,25},{2,10},{10,18},{18,26},{... | collective-permute-start | bytes 1572872 | tf_op jit(solution)/shard_map/while/body/eval_jaxpr/ppermute | solution.py:25
  202.3 28.0 %collective-permute-start = (f32[1,2,256,256]{3,2,1,0:T(8,128)}, f32[1,2,256,256]{3,2,1,0:T(8,128)S(1)}, u32[]{:S(2)}, u32[]{:S(2)}) collective-permute-start(f32[1,2,256,256]{3,2,1,0:T(8,128)} %get-tuple-element.1993), channel_id=1, source_target_pairs={{0,8},{8,16},{16,24},{1,9},{9,17},{17,25},{2,10},{10,18},{18,26},{... | collective-permute-start | bytes 1572872 | tf_op jit(solution)/shard_map/while/body/eval_jaxpr/ppermute | solution.py:25
  247.4 20.4 %collective-permute-start.1 = (f32[1,2,256,256]{3,2,1,0:T(8,128)}, f32[1,2,256,256]{3,2,1,0:T(8,128)S(1)}, u32[]{:S(2)}, u32[]{:S(2)}) collective-permute-start(f32[1,2,256,256]{3,2,1,0:T(8,128)} %get-tuple-element.2007), channel_id=1, source_target_pairs={{8,0},{16,8},{24,16},{9,1},{17,9},{25,17},{10,2},{18,10},{26,18},{... | collective-permute-start | bytes 1572872 | tf_op jit(solution)/shard_map/while/body/eval_jaxpr/ppermute | solution.py:25
  270.1 29.4 %collective-permute-start.1 = (f32[1,2,256,256]{3,2,1,0:T(8,128)}, f32[1,2,256,256]{3,2,1,0:T(8,128)S(1)}, u32[]{:S(2)}, u32[]{:S(2)}) collective-permute-start(f32[1,2,256,256]{3,2,1,0:T(8,128)} %get-tuple-element.2007), channel_id=1, source_target_pairs={{8,0},{16,8},{24,16},{9,1},{17,9},{25,17},{10,2},{18,10},{26,18},{... | collective-permute-start | bytes 1572872 | tf_op jit(solution)/shard_map/while/body/eval_jaxpr/ppermute | solution.py:25
  301.8 88.9 %collective-permute-start.1 = (f32[1,2,256,256]{3,2,1,0:T(8,128)}, f32[1,2,256,256]{3,2,1,0:T(8,128)S(1)}, u32[]{:S(2)}, u32[]{:S(2)}) collective-permute-start(f32[1,2,256,256]{3,2,1,0:T(8,128)} %get-tuple-element.2007), channel_id=1, source_target_pairs={{8,0},{16,8},{24,16},{9,1},{17,9},{25,17},{10,2},{18,10},{26,18},{... | collective-permute-start | bytes 1572872 | tf_op jit(solution)/shard_map/while/body/eval_jaxpr/ppermute | solution.py:25
  406.3 20.1 %collective-permute-start.1 = (f32[1,2,256,256]{3,2,1,0:T(8,128)}, f32[1,2,256,256]{3,2,1,0:T(8,128)S(1)}, u32[]{:S(2)}, u32[]{:S(2)}) collective-permute-start(f32[1,2,256,256]{3,2,1,0:T(8,128)} %get-tuple-element.2007), channel_id=1, source_target_pairs={{8,0},{16,8},{24,16},{9,1},{17,9},{25,17},{10,2},{18,10},{26,18},{... | collective-permute-start | bytes 1572872 | tf_op jit(solution)/shard_map/while/body/eval_jaxpr/ppermute | solution.py:25
  442.1 10.1 %collective-permute-start.1 = (f32[1,2,256,256]{3,2,1,0:T(8,128)}, f32[1,2,256,256]{3,2,1,0:T(8,128)S(1)}, u32[]{:S(2)}, u32[]{:S(2)}) collective-permute-start(f32[1,2,256,256]{3,2,1,0:T(8,128)} %get-tuple-element.2007), channel_id=1, source_target_pairs={{8,0},{16,8},{24,16},{9,1},{17,9},{25,17},{10,2},{18,10},{26,18},{... | collective-permute-start | bytes 1572872 | tf_op jit(solution)/shard_map/while/body/eval_jaxpr/ppermute | solution.py:25
  452.4 6.1 %copy-start.1 = (s32[2]{0:T(128)S(1)}, s32[2]{0:T(128)}, u32[]{:S(2)}) copy-start(s32[2]{0:T(128)} %get-tuple-element.2129) | copy-start | bytes 28
  452.4 6.1 %copy-start.2 = (s32[2]{0:T(128)S(1)}, s32[2]{0:T(128)}, u32[]{:S(2)}) copy-start(s32[2]{0:T(128)} %get-tuple-element.2130) | copy-start | bytes 28
  502.2 64.4 %collective-permute-start.4 = (f32[2,2,256,1024]{3,2,1,0:T(8,128)S(1)}, f32[2,2,256,1024]{3,2,1,0:T(8,128)S(1)}, u32[]{:S(2)}, u32[]{:S(2)}) collective-permute-start(f32[2,2,256,1024]{3,2,1,0:T(8,128)S(1)} %get-tuple-element.1791), channel_id=1, source_target_pairs={{1,0},{2,1},{3,2},{4,3},{5,4},{6,5},{7,6},{9,8},{10,9},{11,10},{12... | collective-permute-start | bytes 12582920 | tf_op jit(solution)/shard_map/ppermute | solution.py:25
  504.1 63.7 %collective-permute-start.5 = (f32[2,2,256,1024]{3,2,1,0:T(8,128)S(1)}, f32[2,2,256,1024]{3,2,1,0:T(8,128)S(1)}, u32[]{:S(2)}, u32[]{:S(2)}) collective-permute-start(f32[2,2,256,1024]{3,2,1,0:T(8,128)S(1)} %get-tuple-element.1792), channel_id=1, source_target_pairs={{0,1},{1,2},{2,3},{3,4},{4,5},{5,6},{6,7},{8,9},{9,10},{10,11},{11... | collective-permute-start | bytes 12582920 | tf_op jit(solution)/shard_map/ppermute | solution.py:25
where the time goes:
time: 576 us; the launch traced here: 574 us
  waiting for transfers between devices  275 us (48%)
  local copies, waits for them, and re-layouts  91.7 us (16%)
  starting transfers between devices  89.1 us (15%)
  matrix products  54.2 us (9%)
  other arithmetic  39.6 us (7%)
  loops' own time  23.3 us (4%)
    ppermute x12, waiting for transfers between devices, passed_along(): lax.ppermute(value, axis, [(source, source + steps) for source in range(i...  231 us
    ppermute x12, starting transfers between devices, passed_along(): lax.ppermute(value, axis, [(source, source + steps) for source in range(i...  82.5 us
    dot_general x96, matrix products, matmul_exact(): return jnp.matmul(left, right, precision=lax.Precision.HIGHEST)  54.2 us
    ppermute x1, waiting for transfers between devices, with_halo(): before = lax.ppermute(last, axis, up)  40.3 us
    dynamic_update_slice x2, local copies, waits for them, and re-layouts, deposit(): return lax.dynamic_update_slice(total, current + placed[position], start)  24.2 us
    another operation x1, loops' own time, local(): lax.fori_loop(0, step_count, forward_turn, (jnp.zeros(shape_block, jnp.fl...  13.5 us
  transfers between devices with their start and end apart: 14, of which 14 were waited for; matrix products, arithmetic and copies ran while one was open for 3% of the time, Pallas kernels for 0%

commit v1 on v0

v1 whole, which is shorter than its diff:
```python
import functools
import math

import jax
import jax.numpy as jnp
import ml_dtypes
import numpy as np
from jax import lax
from jax.experimental import pallas as pl
from jax.experimental.pallas import tpu as pltpu
from jax.sharding import PartitionSpec as P


def dft_tables(length):
    counter = np.arange(length)
    angle = (counter[:, None] * counter[None, :] % length) * (2.0 * math.pi / length)
    cosine, sine = np.cos(angle) / math.sqrt(length), np.sin(angle) / math.sqrt(length)
    values = np.stack([cosine, cosine + sine, cosine - sine])
    high = values.astype(ml_dtypes.bfloat16)
    low = (values - high.astype(np.float64)).astype(ml_dtypes.bfloat16)
    return jnp.asarray(np.stack([high, low]))


def split(x):
    high = x.astype(jnp.bfloat16)
    low = (x - high.astype(jnp.float32)).astype(jnp.bfloat16)
    return high, low


def dot(a, b):
    return jnp.dot(a, b, preferred_element_type=jnp.float32)


def three_dot(a, b):
    return dot(a[0], b[0]) + (dot(a[0], b[1]) + dot(a[1], b[0]))


def side(re, im, tables, inverse, left):
    def table(i):
        return tables[0, i], tables[1, i]

    def product(x, i):
        x = split(x)
        return three_dot(table(i), x) if left else three_dot(x, table(i))

    first, second = (2, 1) if inverse else (1, 2)
    both = product(re + im, 0)
    return both - product(im, second), both - product(re, first)


def transform(re, im, tables, inverse):
    re, im = side(re, im, tables, inverse, False)
    return side(re, im, tables, inverse, True)


def inverse_transform(re, im, tables):
    re, im = side(re, im, tables, True, True)
    return side(re, im, tables, True, False)


def wave_kernel(active_ref, probe, wave_table, tables, measured, patches, terms, psi, held):
    count = patches.shape[0]

    @pl.when(active_ref[0] == 1)
    def _():
        held[0] = probe[0]
        held[1] = probe[1]

        def exit_wave(s):
            a, b = held[0], held[1]
            psi[s, 0] = a
            psi[s, 1] = b
            c, d = patches[s, 0], patches[s, 1]
            return c * a - d * b, c * b + d * a

        def propagate(re, im, sign):
            re, im = transform(re, im, tables, False)
            hr, hi = wave_table[0], wave_table[1]
            if sign > 0:
                re, im = hr * re - hi * im, hr * im + hi * re
            else:
                re, im = hr * re + hi * im, hr * im - hi * re
            re, im = inverse_transform(re, im, tables)
            held[0] = re
            held[1] = im

        @pl.loop(0, count - 1)
        def _(s):
            re, im = exit_wave(s)
            propagate(re, im, 1)

        re, im = exit_wave(count - 1)
        re, im = transform(re, im, tables, False)
        misfit = re * re + im * im - measured[...]
        re, im = inverse_transform(misfit * re, misfit * im, tables)
        held[0] = re
        held[1] = im

        def term(s):
            a, b = held[0], held[1]
            c, d = psi[s, 0], psi[s, 1]
            terms[s, 0] = c * a + d * b
            terms[s, 1] = c * b - d * a
            return a, b

        @pl.loop(0, count - 1)
        def _(i):
            s = count - 1 - i
            a, b = term(s)
            c, d = patches[s, 0], patches[s, 1]
            propagate(c * a + d * b, c * b - d * a, -1)

        term(0)


def local(probe, prop_phase, object_field, measured, offsets):
    width = probe.shape[-1]
    slab = object_field.shape[1]
    columns = object_field.shape[3]
    blocks = columns // width
    owned = offsets.shape[0]
    depth_count = lax.axis_size("depth")
    lat_count = lax.axis_size("lat")
    depth = lax.axis_index("depth")
    lat = lax.axis_index("lat")
    tables = dft_tables(width)
    wave_table = jnp.stack([jnp.cos(prop_phase), jnp.sin(prop_phase)])
    rows = lax.broadcasted_iota(jnp.int32, (width, width), 0)
    lanes = lax.broadcasted_iota(jnp.int32, (width, width), 1)

    up = [(i, i + 1) for i in range(lat_count - 1)]
    down = [(i + 1, i) for i in range(lat_count - 1)]
    offsets_below = lax.ppermute(offsets, "lat", up)
    offsets_above = lax.ppermute(offsets, "lat", down)

    def row_mask(row):
        start = row - lat * width
        return (rows >= start) & (rows < start + width)

    def piece(offset):
        mask = row_mask(offset[0])
        block = offset[1] // width
        rest = offset[1] % width
        zero = jnp.zeros((), jnp.int32)
        shape = object_field.shape[:3] + (width,)
        first = lax.dynamic_slice(object_field, (zero, zero, zero, block * width), shape)
        block = jnp.minimum(block + 1, blocks - 1)
        second = lax.dynamic_slice(object_field, (zero, zero, zero, block * width), shape)
        return jnp.where(mask, jnp.where(lanes >= rest, first, second), 0.0)

    def pieces(of):
        return jnp.stack([piece(of[i]) for i in range(owned)])

    from_below = lax.ppermute(pieces(offsets_above), "lat", up)
    from_above = lax.ppermute(pieces(offsets_below), "lat", down)
    mine = pieces(offsets) + from_below + from_above

    names = ("depth", "lat")

    def pairs(step, back):
        out = []
        for k in range(lat_count):
            for p in range(owned):
                e = (k * owned + p) % depth_count
                d = (e + step) % depth_count
                pair = (d * lat_count + k, e * lat_count + k)
                out.append(pair[::-1] if back else pair)
        return out

    def slot(e):
        return (e - lat * owned) % depth_count

    mine_slot = slot(depth)
    active = mine_slot < owned
    position = jnp.minimum(mine_slot, owned - 1)

    def of_position(array, p):
        return lax.dynamic_index_in_dim(array, jnp.minimum(p, owned - 1), 0, keepdims=False)

    parts = jnp.zeros((depth_count, 2, slab, width, width), jnp.float32)
    parts = lax.dynamic_update_index_in_dim(parts, of_position(mine, mine_slot), depth, 0)
    for step in range(1, depth_count):
        target = (depth - step) % depth_count
        got = lax.ppermute(of_position(mine, slot(target)), names, pairs(step, False))
        parts = lax.dynamic_update_index_in_dim(parts, got, (depth + step) % depth_count, 0)
    patches = jnp.transpose(parts, (0, 2, 1, 3, 4)).reshape(-1, 2, width, width)

    offset = of_position(offsets, mine_slot)
    rolled = jnp.roll(probe, (offset[0] % width, offset[1] % width), (1, 2))
    terms = pl.pallas_call(
        wave_kernel,
        out_shape=jax.ShapeDtypeStruct(patches.shape, jnp.float32),
        in_specs=[pl.BlockSpec(memory_space=pltpu.SMEM)]
        + [pl.BlockSpec(memory_space=pltpu.VMEM)] * 5,
        out_specs=pl.BlockSpec(memory_space=pltpu.VMEM),
        scratch_shapes=[
            pltpu.VMEM(patches.shape, jnp.float32),
            pltpu.VMEM(patches.shape[1:], jnp.float32),
        ],
        compiler_params=pltpu.CompilerParams(vmem_limit_bytes=48 * 1024 * 1024),
    )(
        active.astype(jnp.int32)[None],
        rolled,
        wave_table,
        tables,
        of_position(measured, mine_slot),
        patches,
    )
    terms = jnp.transpose(terms.reshape(depth_count, slab, 2, width, width), (0, 2, 1, 3, 4))

    zero_terms = jnp.zeros((owned, 2, slab, width, width), jnp.float32)
    own = lax.dynamic_index_in_dim(terms, depth, 0, keepdims=False)
    total_terms = [jnp.where(mine_slot == p, own, 0.0) for p in range(owned)]
    for step in range(1, depth_count):
        target = (depth + step) % depth_count
        got = lax.ppermute(
            lax.dynamic_index_in_dim(terms, target, 0, keepdims=False), names, pairs(step, True)
        )
        source = slot((depth - step) % depth_count)
        total_terms = [jnp.where(source == p, got, t) for p, t in enumerate(total_terms)]
    mine_terms = jnp.stack(total_terms)
    terms_below = lax.ppermute(mine_terms, "lat", up)
    terms_above = lax.ppermute(mine_terms, "lat", down)

    total = [jnp.zeros(object_field.shape[:3] + (width,), jnp.float32) for _ in range(blocks)]
    sources = ((offsets, mine_terms), (offsets_below, terms_below), (offsets_above, terms_above))
    for rank, (of, values) in enumerate(sources):
        exists = (lat > 0) if rank == 1 else (lat < lat_count - 1) if rank == 2 else True
        for p in range(owned):
            mask = row_mask(of[p, 0]) & exists
            block = of[p, 1] // width
            rest = of[p, 1] % width
            for b in range(blocks):
                here = ((block == b) & (lanes >= rest)) | ((block + 1 == b) & (lanes < rest))
                total[b] = total[b] + jnp.where(mask & here, values[p], 0.0)
    return jnp.concatenate(total, axis=3)


def solution(mesh):
    in_specs = (P(), P(), P(None, "depth", "lat", None), P("lat", None, None), P("lat", None))
    out_specs = P(None, "depth", "lat", None)
    return jax.shard_map(local, mesh=mesh, in_specs=in_specs, out_specs=out_specs, check_vma=False)
```

time: 576 us -> 226 us (0.39)
  waiting for transfers between devices: 275 us -> 124 us
  local copies, waits for them, and re-layouts: 91.7 us -> 13.9 us
  starting transfers between devices: 89.1 us -> 29.2 us
  matrix products: 54.2 us -> 0 us
  loops' own time: 23.3 us -> 0 us
  between operations: 0.42 us -> 23.3 us
  other arithmetic: 39.6 us -> 31.1 us
    ppermute x14 -> x12, waiting for transfers between devices: 275 us -> 124 us  [the longest x3 57.1 us: local(): lax.ppermute(lax.dynamic_index_in_dim(terms, target, 0, keepdims=False),...]
    ppermute x14 -> x12, starting transfers between devices: 89.1 us -> 29.2 us  [the longest x3 6.84 us: local(): lax.ppermute(of_position(mine, slot(target)), names, pairs(step, False))]
    dot_general x96 -> x0, matrix products: 54.2 us -> none  [matmul_exact(): return jnp.matmul(left, right, precision=lax.Precision.HIGHEST)]
    dynamic_update_slice x17 -> x4, local copies, waits for them, and re-layouts: 38.8 us -> 1.57 us  [the longest x3 1.49 us: local(): lax.dynamic_update_index_in_dim(parts, got, (depth + step) % depth_count, 0)]
    another operation x20 -> x0, loops' own time: 23.3 us -> none  [the longest x1 13.5 us: local(): lax.fori_loop(0, step_count, forward_turn, (jnp.zeros(shape_block, jnp.fl...]
    dynamic_slice x15 -> x2, local copies, waits for them, and re-layouts: 15.9 us -> 2.62 us  [the longest x1 2.62 us: local(): own = lax.dynamic_index_in_dim(terms, depth, 0, keepdims=False)]
    broadcast_in_dim x4 -> x1, local copies, waits for them, and re-layouts: 10.2 us -> 0.4 us  [local(): parts = jnp.zeros((depth_count, 2, slab, width, width), jnp.float32)]
    gather x6 -> x0, local copies, waits for them, and re-layouts: 9.57 us -> none
  transfers between devices with their start and end apart: 14 -> 12, of which waited for: 14 -> 7; matrix products, arithmetic and copies ran while one was open for 3% -> 6% of each run, Pallas kernels for 0% -> 0%
where the time goes in v1:
time: 226 us; the launch traced here: 225 us
  waiting for transfers between devices  124 us (55%)
  other arithmetic  31.1 us (14%)
  starting transfers between devices  29.2 us (13%)
  between operations  23.3 us (10%)
  local copies, waits for them, and re-layouts  13.9 us (6%)
  Pallas kernels  4.16 us (2%)
    ppermute x3, waiting for transfers between devices, local(): lax.ppermute(lax.dynamic_index_in_dim(terms, target, 0, keepdims=False),...  57.1 us
    ppermute x3, waiting for transfers between devices, local(): lax.ppermute(of_position(mine, slot(target)), names, pairs(step, False))  19.3 us
    ppermute x1, waiting for transfers between devices, local(): terms_below = lax.ppermute(mine_terms, 'lat', up)  18.2 us
    ppermute x1, waiting for transfers between devices, local(): from_below = lax.ppermute(pieces(offsets_above), 'lat', up)  14.6 us
    add x4, other arithmetic, local(): total[b] = total[b] + jnp.where(mask & here, values[p], 0.0)  10.6 us
    ppermute x1, waiting for transfers between devices, local(): from_above = lax.ppermute(pieces(offsets_below), 'lat', down)  10 us
    another operation x4, other arithmetic, pieces(): return jnp.stack([piece(of[i]) for i in range(owned)])  9.58 us
    ppermute x3, starting transfers between devices, local(): lax.ppermute(of_position(mine, slot(target)), names, pairs(step, False))  6.84 us
  transfers between devices with their start and end apart: 12, of which 7 were waited for; matrix products, arithmetic and copies ran while one was open for 6% of the time, Pallas kernels for 0%

profile of v1, /device:TPU:1, one launch (start us, length us, event | category | flops | bytes accessed | tf_op | source)
XLA Modules:
  0.0 225.1 jit_solution(3713338674475167912)
XLA Ops:
  0.0 2.1 collective-permute-start
  2.1 4.6 %collective-permute-start.2 = (s32[2,2]{1,0:T(2,128)}, s32[2,2]{1,0:T(2,128)S(1)}, u32[]{:S(2)}, u32[]{:S(2)}) collective-permute-start(s32[2,2]{1,0:T(2,128)} %param.10), channel_id=1, source_target_pairs={{0,1},{1,2},{2,3},{3,4},{4,5},{5,6},{6,7},{8,9},{9,10},{10,11},{11... | collective-permute-start | bytes 56 | tf_op jit(solution)/shard_map/ppermute | solution.py:133
  6.7 1.4 fusion.7
  27.1 4.1 %select_bitcast_fusion.5 = (f32[1,2,2,256,256]{4,3,2,1,0:T(8,128)S(1)}, f32[1,2,2,256,256]{4,3,2,1,0:T(8,128)S(1)}, f32[1,2,2,256,256]{4,3,2,1,0:T(8,128)S(1)}, f32[1,2,2,256,256]{4,3,2,1,0:T(8,128)S(1)}) fusion(f32[2,2,256,1024]{3,2,1,0:T(8,128)} %param.8, s32[]{:T(128)S(6)} %select_n.411, s32[]{:T(128)S(6)} %select_n.410, ...), kind=kLoop, calls=%fused_computation.39 | loop fusion | flops 2097152 | bytes 12584992 | tf_op jit(solution)/shard_map/stack | solution.py:152
  31.2 1.5 pad_maximum_fusion.1
  32.7 2.5 %collective-permute-start.1 = (f32[2,2,2,256,256]{4,3,2,1,0:T(8,128)}, f32[2,2,2,256,256]{4,3,2,1,0:T(8,128)}, u32[]{:S(2)}, u32[]{:S(2)}) collective-permute-start(f32[2,2,2,256,256]{4,3,2,1,0:T(8,128)} %pad_maximum_fusion.1), channel_id=1, source_target_pairs={{0,1},{1,2},{2,3},{3,4},{4,5},{5,6},{6,7},{8,9},{9,10},{10,11},{11... | collective-permute-start | bytes 6291464 | tf_op jit(solution)/shard_map/ppermute | solution.py:154
  36.5 2.5 %select_bitcast_fusion.1 = (f32[1,2,2,256,256]{4,3,2,1,0:T(8,128)S(1)}, f32[1,2,2,256,256]{4,3,2,1,0:T(8,128)S(1)}) fusion(f32[2,2,256,1024]{3,2,1,0:T(8,128)} %param.8, s32[]{:T(128)S(6)} %select_n.435, s32[]{:T(128)S(6)} %select_n.434, pred[256]{0:T(512)(128)(4,1)S(1)} %get-tuple-element.70, pred[256]{0:T(512)(128)(4,1)S(1)} %get-tuple-element.80, ...), kind=kLoop, calls=%fused_computation.35 | loop fusion | flops 1048576 | bytes 6292496 | tf_op jit(solution)/shard_map/stack | solution.py:152
  39.0 1.5 pad_maximum_fusion.2
  40.5 3.2 %collective-permute-start.3 = (f32[2,2,2,256,256]{4,3,2,1,0:T(8,128)}, f32[2,2,2,256,256]{4,3,2,1,0:T(8,128)}, u32[]{:S(2)}, u32[]{:S(2)}) collective-permute-start(f32[2,2,2,256,256]{4,3,2,1,0:T(8,128)} %pad_maximum_fusion.2), channel_id=1, source_target_pairs={{1,0},{2,1},{3,2},{4,3},{5,4},{6,5},{7,6},{9,8},{10,9},{11,10},{12... | collective-permute-start | bytes 6291464 | tf_op jit(solution)/shard_map/ppermute | solution.py:155
  43.8 14.6 %collective-permute-done.1 = f32[2,2,2,256,256]{4,3,2,1,0:T(8,128)} collective-permute-done((f32[2,2,2,256,256]{4,3,2,1,0:T(8,128)}, f32[2,2,2,256,256]{4,3,2,1,0:T(8,128)}, u32[]{:S(2)}, u32[]{:S(2)}) %collective-permute-start.1) | collective-permute-done | bytes 2097184 | tf_op jit(solution)/shard_map/ppermute | solution.py:154
  58.4 10.0 %collective-permute-done.3 = f32[2,2,2,256,256]{4,3,2,1,0:T(8,128)} collective-permute-done((f32[2,2,2,256,256]{4,3,2,1,0:T(8,128)}, f32[2,2,2,256,256]{4,3,2,1,0:T(8,128)}, u32[]{:S(2)}, u32[]{:S(2)}) %collective-permute-start.3) | collective-permute-done | bytes 2097184 | tf_op jit(solution)/shard_map/ppermute | solution.py:155
  68.4 2.6 %fusion = f32[2,2,2,256,256]{4,3,2,1,0:T(8,128)S(1)} fusion(f32[2,2,2,256,256]{4,3,2,1,0:T(8,128)} %collective-permute-done.3, f32[2,2,2,256,256]{4,3,2,1,0:T(8,128)} %collective-permute-done.1, f32[1,2,2,256,256]{4,3,2,1,0:T(8,128)S(1)} %get-tuple-element.20, f32[1,2,2,256,256]{4,3,2,1,0:T(8,128)S(1)} %get-tuple-element.19), kind=kLoop, calls=%fused_computation.2 | loop fusion | flops 1572864 | bytes 8388608 | tf_op jit(solution)/shard_map/add | solution.py:156
  71.1 1.8 dynamic-slice_bitcast_fusion
  72.9 4.8 %collective-permute-start.4 = (f32[2,2,256,256]{3,2,1,0:T(8,128)}, f32[2,2,256,256]{3,2,1,0:T(8,128)}, u32[]{:S(2)}, u32[]{:S(2)}) collective-permute-start(f32[2,2,256,256]{3,2,1,0:T(8,128)} %get-tuple-element.27), channel_id=1, source_target_pairs={{8,0},{16,8},{25,17},{1,25},{10,2},{18,10},{27,19},{3,27},{12,4},{... | collective-permute-start | bytes 3145736 | tf_op jit(solution)/shard_map/ppermute | solution.py:184
  86.0 2.8 %collective-permute-done.4 = f32[2,2,256,256]{3,2,1,0:T(8,128)} collective-permute-done((f32[2,2,256,256]{3,2,1,0:T(8,128)}, f32[2,2,256,256]{3,2,1,0:T(8,128)}, u32[]{:S(2)}, u32[]{:S(2)}) %collective-permute-start.4) | collective-permute-done | bytes 1048608 | tf_op jit(solution)/shard_map/ppermute | solution.py:184
  90.0 16.5 %collective-permute-done.5 = f32[2,2,256,256]{3,2,1,0:T(8,128)S(1)} collective-permute-done((f32[2,2,256,256]{3,2,1,0:T(8,128)}, f32[2,2,256,256]{3,2,1,0:T(8,128)S(1)}, u32[]{:S(2)}, u32[]{:S(2)}) %collective-permute-start.5) | collective-permute-done | bytes 1048608 | tf_op jit(solution)/shard_map/ppermute | solution.py:184
  106.8 2.0 copy-done.3
  108.8 4.2 %shard_map.64 = f32[8,2,256,256]{3,2,1,0:T(8,128)} custom-call(s32[1]{0:T(128)} %bitcast.2.active_ref, f32[2,256,256]{2,1,0:T(8,128)S(1)} %get-tuple-element.105.probe, f32[2,256,256]{2,1,0:T(8,128)S(1)} %get-tuple-element.106.wave_table, bf16[2,3,256,256]{3,2,1,0:T(8,128)(2,1)S(1)} %copy-done.2, f32[256,256]{1,0:T(8,128)S(1)} %dynamic-slice_bitcast_fusion.3.measured, ...), custom_call_target="tpu_custom_call" | custom-call | tf_op jit(solution)/shard_map/pallas_call | solution.py:190
  113.0 2.6 %constant_dynamic-slice_fusion = (f32[1,2,2,256,256]{4,3,2,1,0:T(8,128)S(1)}, f32[1,2,2,256,256]{4,3,2,1,0:T(8,128)S(1)}, f32[1,2,2,256,256]{4,3,2,1,0:T(8,128)S(1)}, f32[1,2,2,256,256]{4,3,2,1,0:T(8,128)S(1)}) fusion(f32[4,2,2,256,256]{4,3,2,1,0:T(8,128)} %bitcast.127, s32[]{:T(128)S(6)} %select_n.444, s32[]{:T(128)S(6)} %select_n.449, s32[]{:T(128)S(6)} %select_n.454, ...), kind=kLoop, calls=%fused_computation.70 | loop fusion | bytes 8388624 | tf_op jit(solution)/shard_map/jit(dynamic_index_in_dim)/dynamic_slice | solution.py:212
  115.7 1.7 collective-permute-start.7
  121.4 57.1 %collective-permute-done.8 = f32[2,2,256,256]{3,2,1,0:T(8,128)} collective-permute-done((f32[2,2,256,256]{3,2,1,0:T(8,128)S(1)}, f32[2,2,256,256]{3,2,1,0:T(8,128)}, u32[]{:S(2)}, u32[]{:S(2)}) %collective-permute-start.8) | collective-permute-done | bytes 1048608 | tf_op jit(solution)/shard_map/ppermute | solution.py:216
  178.5 2.2 fusion.4
  180.7 1.6 pad_maximum_fusion.3
  182.2 1.9 collective-permute-start.10
  184.1 3.9 %collective-permute-start.11 = (f32[2,2,2,256,256]{4,3,2,1,0:T(8,128)}, f32[2,2,2,256,256]{4,3,2,1,0:T(8,128)}, u32[]{:S(2)}, u32[]{:S(2)}) collective-permute-start(f32[2,2,2,256,256]{4,3,2,1,0:T(8,128)} %pad_maximum_fusion.3), channel_id=1, source_target_pairs={{1,0},{2,1},{3,2},{4,3},{5,4},{6,5},{7,6},{9,8},{10,9},{11,10},{12... | collective-permute-start | bytes 6291464 | tf_op jit(solution)/shard_map/ppermute | solution.py:223
  189.3 18.2 %collective-permute-done.10 = f32[2,2,2,256,256]{4,3,2,1,0:T(8,128)} collective-permute-done((f32[2,2,2,256,256]{4,3,2,1,0:T(8,128)}, f32[2,2,2,256,256]{4,3,2,1,0:T(8,128)}, u32[]{:S(2)}, u32[]{:S(2)}) %collective-permute-start.10) | collective-permute-done | bytes 2097184 | tf_op jit(solution)/shard_map/ppermute | solution.py:222
  207.4 4.4 %collective-permute-done.11 = f32[2,2,2,256,256]{4,3,2,1,0:T(8,128)} collective-permute-done((f32[2,2,2,256,256]{4,3,2,1,0:T(8,128)}, f32[2,2,2,256,256]{4,3,2,1,0:T(8,128)}, u32[]{:S(2)}, u32[]{:S(2)}) %collective-permute-start.11) | collective-permute-done | bytes 2097184 | tf_op jit(solution)/shard_map/ppermute | solution.py:223
  211.8 2.7 %select_add_fusion.3 = f32[2,2,256,256]{3,2,1,0:T(8,128)S(1)} fusion(f32[2,2,256,256]{3,2,1,0:T(8,128)S(1)} %get-tuple-element.14, f32[2,2,256,256]{3,2,1,0:T(8,128)S(1)} %get-tuple-element.13, f32[2,2,2,256,256]{4,3,2,1,0:T(8,128)} %collective-permute-done.10, f32[2,2,2,256,256]{4,3,2,1,0:T(8,128)} %collective-permute-done.11, ...), kind=kLoop, calls=%fused_computation.30 | loop fusion | flops 2883584 | bytes 7733248 | tf_op jit(solution)/shard_map/add | solution.py:235
  214.5 2.7 %select_add_fusion.2 = f32[2,2,256,256]{3,2,1,0:T(8,128)S(1)} fusion(f32[2,2,256,256]{3,2,1,0:T(8,128)S(1)} %get-tuple-element.14, f32[2,2,256,256]{3,2,1,0:T(8,128)S(1)} %get-tuple-element.13, f32[2,2,2,256,256]{4,3,2,1,0:T(8,128)} %collective-permute-done.10, f32[2,2,2,256,256]{4,3,2,1,0:T(8,128)} %collective-permute-done.11, ...), kind=kLoop, calls=%fused_computation.29 | loop fusion | flops 2883584 | bytes 7733248 | tf_op jit(solution)/shard_map/add | solution.py:235
  217.1 2.7 %select_add_fusion.1 = f32[2,2,256,256]{3,2,1,0:T(8,128)S(1)} fusion(f32[2,2,256,256]{3,2,1,0:T(8,128)S(1)} %get-tuple-element.14, f32[2,2,256,256]{3,2,1,0:T(8,128)S(1)} %get-tuple-element.13, f32[2,2,2,256,256]{4,3,2,1,0:T(8,128)} %collective-permute-done.10, f32[2,2,2,256,256]{4,3,2,1,0:T(8,128)} %collective-permute-done.11, ...), kind=kLoop, calls=%fused_computation.28 | loop fusion | flops 2883584 | bytes 7733248 | tf_op jit(solution)/shard_map/add | solution.py:235
  219.8 2.7 %select_add_fusion = f32[2,2,256,256]{3,2,1,0:T(8,128)S(1)} fusion(f32[2,2,256,256]{3,2,1,0:T(8,128)S(1)} %get-tuple-element.14, f32[2,2,256,256]{3,2,1,0:T(8,128)S(1)} %get-tuple-element.13, f32[2,2,2,256,256]{4,3,2,1,0:T(8,128)} %collective-permute-done.10, f32[2,2,2,256,256]{4,3,2,1,0:T(8,128)} %collective-permute-done.11, ...), kind=kLoop, calls=%fused_computation.27 | loop fusion | flops 2883584 | bytes 7733248 | tf_op jit(solution)/shard_map/add | solution.py:235
  222.5 2.7 %pad_maximum_fusion = f32[2,2,256,1024]{3,2,1,0:T(8,128)} fusion(f32[2,2,256,256]{3,2,1,0:T(8,128)S(1)} %select_add_fusion, f32[2,2,256,256]{3,2,1,0:T(8,128)S(1)} %select_add_fusion.1, f32[2,2,256,256]{3,2,1,0:T(8,128)S(1)} %select_add_fusion.2, f32[2,2,256,256]{3,2,1,0:T(8,128)S(1)} %select_add_fusion.3), kind=kLoop, calls=%fused_computation | loop fusion | flops 3145728 | bytes 8388608 | tf_op jit(solution)/shard_map/concatenate | solution.py:236
  (62 shorter events, 12.6 us)
Async XLA Ops:
  0.0 85.1 %copy-start = (f32[2,256,256]{2,1,0:T(8,128)S(1)}, f32[2,256,256]{2,1,0:T(8,128)}, u32[]{:S(2)}) copy-start(f32[2,256,256]{2,1,0:T(8,128)} %param.9) | copy-start | bytes 1572868
  0.0 14.2 %collective-permute-start = (s32[2,2]{1,0:T(2,128)}, s32[2,2]{1,0:T(2,128)S(1)}, u32[]{:S(2)}, u32[]{:S(2)}) collective-permute-start(s32[2,2]{1,0:T(2,128)} %param.10), channel_id=1, source_target_pairs={{1,0},{2,1},{3,2},{4,3},{5,4},{6,5},{7,6},{9,8},{10,9},{11,10},{12... | collective-permute-start | bytes 56 | tf_op jit(solution)/shard_map/ppermute | solution.py:134
  2.1 17.8 %collective-permute-start.2 = (s32[2,2]{1,0:T(2,128)}, s32[2,2]{1,0:T(2,128)S(1)}, u32[]{:S(2)}, u32[]{:S(2)}) collective-permute-start(s32[2,2]{1,0:T(2,128)} %param.10), channel_id=1, source_target_pairs={{0,1},{1,2},{2,3},{3,4},{4,5},{5,6},{6,7},{8,9},{9,10},{10,11},{11... | collective-permute-start | bytes 56 | tf_op jit(solution)/shard_map/ppermute | solution.py:133
  32.7 25.7 %collective-permute-start.1 = (f32[2,2,2,256,256]{4,3,2,1,0:T(8,128)}, f32[2,2,2,256,256]{4,3,2,1,0:T(8,128)}, u32[]{:S(2)}, u32[]{:S(2)}) collective-permute-start(f32[2,2,2,256,256]{4,3,2,1,0:T(8,128)} %pad_maximum_fusion.1), channel_id=1, source_target_pairs={{0,1},{1,2},{2,3},{3,4},{4,5},{5,6},{6,7},{8,9},{9,10},{10,11},{11... | collective-permute-start | bytes 6291464 | tf_op jit(solution)/shard_map/ppermute | solution.py:154
  40.5 28.0 %collective-permute-start.3 = (f32[2,2,2,256,256]{4,3,2,1,0:T(8,128)}, f32[2,2,2,256,256]{4,3,2,1,0:T(8,128)}, u32[]{:S(2)}, u32[]{:S(2)}) collective-permute-start(f32[2,2,2,256,256]{4,3,2,1,0:T(8,128)} %pad_maximum_fusion.2), channel_id=1, source_target_pairs={{1,0},{2,1},{3,2},{4,3},{5,4},{6,5},{7,6},{9,8},{10,9},{11,10},{12... | collective-permute-start | bytes 6291464 | tf_op jit(solution)/shard_map/ppermute | solution.py:155
  71.1 6.6 %copy-start.6 = (s32[2,2]{1,0:T(2,128)S(1)}, s32[2,2]{1,0:T(2,128)}, u32[]{:S(2)}) copy-start(s32[2,2]{1,0:T(2,128)} %param.10) | copy-start | bytes 52
  71.1 10.7 %copy-start.4 = (f32[2,256,256]{2,1,0:T(8,128)S(1)}, f32[2,256,256]{2,1,0:T(8,128)}, u32[]{:S(2)}) copy-start(f32[2,256,256]{2,1,0:T(8,128)} %param.6) | copy-start | bytes 1572868
  71.1 12.3 %copy-start.5 = (f32[256,256]{1,0:T(8,128)S(1)}, f32[256,256]{1,0:T(8,128)}, u32[]{:S(2)}) copy-start(f32[256,256]{1,0:T(8,128)} %param.7) | copy-start | bytes 786436
  72.9 15.9 %collective-permute-start.4 = (f32[2,2,256,256]{3,2,1,0:T(8,128)}, f32[2,2,256,256]{3,2,1,0:T(8,128)}, u32[]{:S(2)}, u32[]{:S(2)}) collective-permute-start(f32[2,2,256,256]{3,2,1,0:T(8,128)} %get-tuple-element.27), channel_id=1, source_target_pairs={{8,0},{16,8},{25,17},{1,25},{10,2},{18,10},{27,19},{3,27},{12,4},{... | collective-permute-start | bytes 3145736 | tf_op jit(solution)/shard_map/ppermute | solution.py:184
  82.0 24.6 %collective-permute-start.5 = (f32[2,2,256,256]{3,2,1,0:T(8,128)}, f32[2,2,256,256]{3,2,1,0:T(8,128)S(1)}, u32[]{:S(2)}, u32[]{:S(2)}) collective-permute-start(f32[2,2,256,256]{3,2,1,0:T(8,128)} %get-tuple-element.26), channel_id=1, source_target_pairs={{16,0},{24,8},{1,17},{9,25},{18,2},{26,10},{3,19},{11,27},{20,4},{... | collective-permute-start | bytes 3145736 | tf_op jit(solution)/shard_map/ppermute | solution.py:184
  84.3 22.3 %collective-permute-start.6 = (f32[2,2,256,256]{3,2,1,0:T(8,128)S(1)}, f32[2,2,256,256]{3,2,1,0:T(8,128)S(1)}, u32[]{:S(2)}, u32[]{:S(2)}) collective-permute-start(f32[2,2,256,256]{3,2,1,0:T(8,128)S(1)} %get-tuple-element.25), channel_id=1, source_target_pairs={{24,0},{0,8},{9,17},{17,25},{26,2},{2,10},{11,19},{19,27},{28,4},{... | collective-permute-start | bytes 3145736 | tf_op jit(solution)/shard_map/ppermute | solution.py:184
  90.0 18.8 %copy-start.2 = (bf16[2,3,256,256]{3,2,1,0:T(8,128)(2,1)S(1)}, bf16[2,3,256,256]{3,2,1,0:T(8,128)(2,1)}, u32[]{:S(2)}) copy-start(bf16[2,3,256,256]{3,2,1,0:T(8,128)(2,1)} %constant.295.clone.tables) | copy-start | bytes 2359300
  106.8 2.0 copy-start.3
  115.7 5.7 %collective-permute-start.7 = (f32[2,2,256,256]{3,2,1,0:T(8,128)S(1)}, f32[2,2,256,256]{3,2,1,0:T(8,128)}, u32[]{:S(2)}, u32[]{:S(2)}) collective-permute-start(f32[2,2,256,256]{3,2,1,0:T(8,128)S(1)} %bitcast.129), channel_id=1, source_target_pairs={{0,24},{8,0},{17,9},{25,17},{2,26},{10,2},{19,11},{27,19},{4,28},{... | collective-permute-start | bytes 3145736 | tf_op jit(solution)/shard_map/ppermute | solution.py:216
  117.4 61.0 %collective-permute-start.8 = (f32[2,2,256,256]{3,2,1,0:T(8,128)S(1)}, f32[2,2,256,256]{3,2,1,0:T(8,128)}, u32[]{:S(2)}, u32[]{:S(2)}) collective-permute-start(f32[2,2,256,256]{3,2,1,0:T(8,128)S(1)} %bitcast.130), channel_id=1, source_target_pairs={{0,16},{8,24},{17,1},{25,9},{2,18},{10,26},{19,3},{27,11},{4,20},{... | collective-permute-start | bytes 3145736 | tf_op jit(solution)/shard_map/ppermute | solution.py:216
  119.8 58.7 %collective-permute-start.9 = (f32[2,2,256,256]{3,2,1,0:T(8,128)}, f32[2,2,256,256]{3,2,1,0:T(8,128)}, u32[]{:S(2)}, u32[]{:S(2)}) collective-permute-start(f32[2,2,256,256]{3,2,1,0:T(8,128)} %bitcast.122), channel_id=1, source_target_pairs={{0,8},{8,16},{17,25},{25,1},{2,10},{10,18},{19,27},{27,3},{4,12},{... | collective-permute-start | bytes 3145736 | tf_op jit(solution)/shard_map/ppermute | solution.py:216
  182.2 25.2 %collective-permute-start.10 = (f32[2,2,2,256,256]{4,3,2,1,0:T(8,128)}, f32[2,2,2,256,256]{4,3,2,1,0:T(8,128)}, u32[]{:S(2)}, u32[]{:S(2)}) collective-permute-start(f32[2,2,2,256,256]{4,3,2,1,0:T(8,128)} %pad_maximum_fusion.3), channel_id=1, source_target_pairs={{0,1},{1,2},{2,3},{3,4},{4,5},{5,6},{6,7},{8,9},{9,10},{10,11},{11... | collective-permute-start | bytes 6291464 | tf_op jit(solution)/shard_map/ppermute | solution.py:222
  184.1 27.7 %collective-permute-start.11 = (f32[2,2,2,256,256]{4,3,2,1,0:T(8,128)}, f32[2,2,2,256,256]{4,3,2,1,0:T(8,128)}, u32[]{:S(2)}, u32[]{:S(2)}) collective-permute-start(f32[2,2,2,256,256]{4,3,2,1,0:T(8,128)} %pad_maximum_fusion.3), channel_id=1, source_target_pairs={{1,0},{2,1},{3,2},{4,3},{5,4},{6,5},{7,6},{9,8},{10,9},{11,10},{12... | collective-permute-start | bytes 6291464 | tf_op jit(solution)/shard_map/ppermute | solution.py:223
  222.5 2.7 %copy-start.1 = (f32[2,256,256]{2,1,0:T(8,128)S(1)}, f32[2,256,256]{2,1,0:T(8,128)}, u32[]{:S(2)}) copy-start(f32[2,256,256]{2,1,0:T(8,128)} %param.9) | copy-start | bytes 1572868

commit v2 on v1

v2 whole, which is shorter than its diff:
```python
import functools
import math

import jax
import jax.numpy as jnp
import ml_dtypes
import numpy as np
from jax import lax
from jax.experimental import pallas as pl
from jax.experimental.pallas import tpu as pltpu
from jax.sharding import PartitionSpec as P


def dft_tables(length):
    counter = np.arange(length)
    angle = (counter[:, None] * counter[None, :] % length) * (2.0 * math.pi / length)
    cosine, sine = np.cos(angle) / math.sqrt(length), np.sin(angle) / math.sqrt(length)
    values = np.stack([cosine, cosine + sine, cosine - sine])
    high = values.astype(ml_dtypes.bfloat16)
    low = (values - high.astype(np.float64)).astype(ml_dtypes.bfloat16)
    return jnp.asarray(np.stack([high, low]))


def split(x):
    high = x.astype(jnp.bfloat16)
    low = (x - high.astype(jnp.float32)).astype(jnp.bfloat16)
    return high, low


def dot(a, b):
    return jnp.dot(a, b, preferred_element_type=jnp.float32)


def three_dot(a, b):
    return dot(a[0], b[0]) + (dot(a[0], b[1]) + dot(a[1], b[0]))


def side(re, im, tables, inverse, left):
    def table(i):
        return tables[0, i], tables[1, i]

    def product(x, i):
        x = split(x)
        return three_dot(table(i), x) if left else three_dot(x, table(i))

    first, second = (2, 1) if inverse else (1, 2)
    both = product(re + im, 0)
    return both - product(im, second), both - product(re, first)


def transform(re, im, tables, inverse):
    re, im = side(re, im, tables, inverse, False)
    return side(re, im, tables, inverse, True)


def inverse_transform(re, im, tables):
    re, im = side(re, im, tables, True, True)
    return side(re, im, tables, True, False)


def row_mask(row, lat, width):
    rows = lax.broadcasted_iota(jnp.int32, (width, width), 0)
    start = row - lat * width
    return (rows >= start) & (rows < start + width)


def extract_kernel(place, offsets, field, mine, to_up, to_down):
    width = field.shape[2]
    blocks = field.shape[3] // width
    lanes = lax.broadcasted_iota(jnp.int32, (width, width), 1)
    for rank, out in enumerate((mine, to_up, to_down)):
        for p in range(mine.shape[0]):
            column = offsets[rank, p, 1]
            block = column // width
            mask = row_mask(offsets[rank, p, 0], place[0], width)
            first = mask & (lanes >= column - block * width)
            second = mask & (lanes < column - block * width)
            after = jnp.minimum(block + 1, blocks - 1)
            for c in range(2):
                a = field[c, 0, :, pl.ds(pl.multiple_of(block * width, width), width)]
                b = field[c, 0, :, pl.ds(pl.multiple_of(after * width, width), width)]
                out[p, 0, c] = jnp.where(first, a, jnp.where(second, b, 0.0))


def deposit_kernel(place, offsets, home, below, above, out):
    width = out.shape[2]
    blocks = out.shape[3] // width
    lanes = lax.broadcasted_iota(jnp.int32, (width, width), 1)
    for b in range(blocks):
        for c in range(2):
            total = jnp.zeros((width, width), jnp.float32)
            for rank, terms in enumerate((home, below, above)):
                for p in range(home.shape[0]):
                    column = offsets[rank, p, 1]
                    block = column // width
                    rest = column - block * width
                    low = jnp.where(block == b, rest, width)
                    high = jnp.where(block + 1 == b, rest, 0)
                    here = (lanes >= low) | (lanes < high)
                    mask = row_mask(offsets[rank, p, 0], place[0], width) & here
                    total += jnp.where(mask, terms[p, 0, c], 0.0)
            out[c, 0, :, b * width : (b + 1) * width] = total


def wave_kernel(
    depth_count, lat_count, probe, wave_table, tables, measured, mine, to_up, to_down,
    home, terms_below, terms_above,
    from_below, from_above, merged, patches, terms, psi, held,
    z_send, z_recv, in_send, in_recv, out_send, out_recv, back_send, back_recv,
):
    depth = lax.axis_index("depth")
    lat = lax.axis_index("lat")
    owned, slab = mine.shape[:2]
    count = depth_count * slab
    has_above = lat < lat_count - 1
    has_below = lat > 0
    slot = lax.rem(depth - lax.rem(lat * owned, depth_count) + depth_count, depth_count)
    active = slot < owned

    def owner(p):
        return lax.rem(lat * owned + p, depth_count)

    barrier = pltpu.get_barrier_semaphore()
    for step in range(1, depth_count):
        other = lax.rem(depth + step, depth_count)
        pl.semaphore_signal(
            barrier, inc=1, device_id=(other, lat), device_id_type=pl.DeviceIdType.MESH
        )

    def greet(other):
        pl.semaphore_signal(
            barrier, inc=1, device_id=(depth, other), device_id_type=pl.DeviceIdType.MESH
        )

    pl.when(has_above)(lambda: greet(lat + 1))
    pl.when(has_below)(lambda: greet(lat - 1))
    peers = depth_count - 1 + has_above.astype(jnp.int32) + has_below.astype(jnp.int32)
    pl.semaphore_wait(barrier, peers)

    def remote(source, target, send, recv, device):
        return pltpu.make_async_remote_copy(
            src_ref=source, dst_ref=target, send_sem=send, recv_sem=recv,
            device_id=device, device_id_type=pl.DeviceIdType.MESH,
        )

    def upward(p, s):
        return remote(to_up.at[p, s], from_below.at[p, s],
                      z_send.at[0, p, s], z_recv.at[0, p, s], (depth, lat + 1))

    def downward(p, s):
        return remote(to_down.at[p, s], from_above.at[p, s],
                      z_send.at[1, p, s], z_recv.at[1, p, s], (depth, lat - 1))

    def inward(p, s):
        place = depth * slab + s
        return remote(merged.at[p, s], patches.at[place],
                      in_send.at[p, s], in_recv.at[place], (owner(p), lat))

    def outward(s):
        layer = lax.rem(s, slab)
        place = jnp.minimum(slot, owned - 1)
        return remote(terms.at[s], home.at[place, layer],
                      out_send.at[s], out_recv.at[place, layer], (s // slab, lat))

    def back_up(p, s):
        return remote(home.at[p, s], terms_below.at[p, s],
                      back_send.at[0, p, s], back_recv.at[0, p, s], (depth, lat + 1))

    def back_down(p, s):
        return remote(home.at[p, s], terms_above.at[p, s],
                      back_send.at[1, p, s], back_recv.at[1, p, s], (depth, lat - 1))

    chunks = [(p, s) for s in range(slab) for p in range(owned)]
    for p, s in chunks:
        pl.when(has_above)(lambda: upward(p, s).start())
        pl.when(has_below)(lambda: downward(p, s).start())
    for p, s in chunks:
        merged[p, s] = mine[p, s]

        @pl.when(has_below)
        def _():
            upward(p, s).wait_recv()
            merged[p, s] += from_below[p, s]

        @pl.when(has_above)
        def _():
            downward(p, s).wait_recv()
            merged[p, s] += from_above[p, s]

        @pl.when(owner(p) == depth)
        def _():
            patches[depth * slab + s] = merged[p, s]

        @pl.when(owner(p) != depth)
        def _():
            inward(p, s).start()

    @pl.when(active)
    def _():
        held[0] = probe[0]
        held[1] = probe[1]

        def exit_wave(s):
            a, b = held[0], held[1]
            psi[s, 0] = a
            psi[s, 1] = b

            @pl.when(s // slab != depth)
            def _():
                remote(merged.at[0, 0], patches.at[s], in_send.at[0, 0],
                       in_recv.at[s], (depth, lat)).wait_recv()

            c, d = patches[s, 0], patches[s, 1]
            return c * a - d * b, c * b + d * a

        def propagate(re, im, sign):
            re, im = transform(re, im, tables, False)
            hr, hi = wave_table[0], wave_table[1]
            if sign > 0:
                re, im = hr * re - hi * im, hr * im + hi * re
            else:
                re, im = hr * re + hi * im, hr * im - hi * re
            re, im = inverse_transform(re, im, tables)
            held[0] = re
            held[1] = im

        @pl.loop(0, count - 1)
        def _(s):
            re, im = exit_wave(s)
            propagate(re, im, 1)

        re, im = exit_wave(count - 1)
        re, im = transform(re, im, tables, False)
        target = measured[0]
        for p in range(1, owned):
            target = jnp.where(slot == p, measured[p], target)
        misfit = re * re + im * im - target
        re, im = inverse_transform(misfit * re, misfit * im, tables)
        held[0] = re
        held[1] = im

        def term(s):
            a, b = held[0], held[1]
            c, d = psi[s, 0], psi[s, 1]
            terms[s, 0] = c * a + d * b
            terms[s, 1] = c * b - d * a

            @pl.when(s // slab != depth)
            def _():
                outward(s).start()

            return a, b

        @pl.loop(0, count - 1)
        def _(i):
            s = count - 1 - i
            a, b = term(s)
            c, d = patches[s, 0], patches[s, 1]
            propagate(c * a + d * b, c * b - d * a, -1)

        term(0)

    back = [(p, s) for s in reversed(range(slab)) for p in range(owned)]
    for p, s in back:

        @pl.when(owner(p) == depth)
        def _():
            home[p, s] = terms[depth * slab + s]

        @pl.when(owner(p) != depth)
        def _():
            remote(terms.at[0], home.at[p, s], out_send.at[0],
                   out_recv.at[p, s], (depth, lat)).wait_recv()

        pl.when(has_above)(lambda: back_up(p, s).start())
        pl.when(has_below)(lambda: back_down(p, s).start())

    for p, s in back:

        @pl.when(has_below)
        def _():
            back_up(p, s).wait_recv()
            downward(p, s).wait_send()
            back_down(p, s).wait_send()

        @pl.when(has_above)
        def _():
            back_down(p, s).wait_recv()
            upward(p, s).wait_send()
            back_up(p, s).wait_send()

        @pl.when(owner(p) != depth)
        def _():
            inward(p, s).wait_send()

    @pl.when(active)
    def _():
        @pl.loop(0, count)
        def _(s):
            @pl.when(s // slab != depth)
            def _():
                outward(s).wait_send()


def local(probe, prop_phase, object_field, measured, offsets):
    width = probe.shape[-1]
    slab, columns = object_field.shape[1], object_field.shape[3]
    owned = offsets.shape[0]
    depth_count = lax.axis_size("depth")
    lat_count = lax.axis_size("lat")
    depth = lax.axis_index("depth")
    lat = lax.axis_index("lat")
    tables = dft_tables(width)
    wave_table = jnp.stack([jnp.cos(prop_phase), jnp.sin(prop_phase)])

    up = [(i, i + 1) for i in range(lat_count - 1)]
    down = [(i + 1, i) for i in range(lat_count - 1)]
    far = -(lat_count + 2) * width
    none = jnp.array([far, 0], jnp.int32) * jnp.ones((owned, 1), jnp.int32)
    below = jnp.where(lat > 0, lax.ppermute(offsets, "lat", up), none)
    above = jnp.where(lat < lat_count - 1, lax.ppermute(offsets, "lat", down), none)
    place = lat.astype(jnp.int32)[None]
    smem = pl.BlockSpec(memory_space=pltpu.SMEM)
    vmem = pl.BlockSpec(memory_space=pltpu.VMEM)
    field_spec = pl.BlockSpec((2, 1, width, columns), lambda s: (0, s, 0, 0))
    piece_spec = pl.BlockSpec((owned, 1, 2, width, width), lambda s: (0, s, 0, 0, 0))
    pieces = jax.ShapeDtypeStruct((owned, slab, 2, width, width), jnp.float32)
    limit = 56 * 1024 * 1024
    mine, to_up, to_down = pl.pallas_call(
        extract_kernel,
        grid=(slab,),
        out_shape=[pieces] * 3,
        in_specs=[smem, smem, field_spec],
        out_specs=[piece_spec] * 3,
        compiler_params=pltpu.CompilerParams(vmem_limit_bytes=limit),
    )(place, jnp.stack([offsets, above, below]), object_field)

    slot = (depth - lat * owned) % depth_count
    offset = lax.dynamic_index_in_dim(offsets, jnp.minimum(slot, owned - 1), 0, keepdims=False)
    rolled = jnp.roll(probe, (offset[0] % width, offset[1] % width), (1, 2))
    layers = (depth_count * slab, 2, width, width)
    dma = pltpu.SemaphoreType.DMA
    home, terms_below, terms_above = pl.pallas_call(
        functools.partial(wave_kernel, depth_count, lat_count),
        out_shape=[pieces] * 3,
        in_specs=[vmem] * 7,
        out_specs=[vmem] * 3,
        scratch_shapes=[pltpu.VMEM(pieces.shape, jnp.float32)] * 3
        + [pltpu.VMEM(layers, jnp.float32)] * 3
        + [
            pltpu.VMEM(layers[1:], jnp.float32),
            dma((2, owned, slab)), dma((2, owned, slab)),
            dma((owned, slab)), dma((layers[0],)),
            dma((layers[0],)), dma((owned, slab)),
            dma((2, owned, slab)), dma((2, owned, slab)),
        ],
        compiler_params=pltpu.CompilerParams(
            vmem_limit_bytes=limit, collective_id=0, has_side_effects=True
        ),
    )(rolled, wave_table, tables, measured, mine, to_up, to_down)

    return pl.pallas_call(
        deposit_kernel,
        grid=(slab,),
        out_shape=jax.ShapeDtypeStruct(object_field.shape, jnp.float32),
        in_specs=[smem, smem] + [piece_spec] * 3,
        out_specs=field_spec,
        compiler_params=pltpu.CompilerParams(vmem_limit_bytes=limit),
    )(place, jnp.stack([offsets, below, above]), home, terms_below, terms_above)


def solution(mesh):
    in_specs = (P(), P(), P(None, "depth", "lat", None), P("lat", None, None), P("lat", None))
    out_specs = P(None, "depth", "lat", None)
    return jax.shard_map(local, mesh=mesh, in_specs=in_specs, out_specs=out_specs, check_vma=False)
```

time: 226 us -> 146 us (0.65)
  Pallas kernels: 4.16 us -> 129 us
  waiting for transfers between devices: 124 us -> 0.01 us
  other arithmetic: 31.1 us -> 3.11 us
  starting transfers between devices: 29.2 us -> 6.63 us
  between operations: 23.3 us -> 4.01 us
  local copies, waits for them, and re-layouts: 13.9 us -> 3.16 us
    pallas_call x1 -> x3, Pallas kernels: 4.16 us -> 129 us  [the longest x1 116 us: local(): pl.pallas_call(functools.partial(wave_kernel, depth_count, lat_count), ou...]
    ppermute x12 -> x2, waiting for transfers between devices: 124 us -> 0.01 us  [the longest x1 0.01 us: local(): below = jnp.where(lat > 0, lax.ppermute(offsets, 'lat', up), none)]
    ppermute x12 -> x2, starting transfers between devices: 29.2 us -> 6.63 us  [the longest x1 4.71 us: local(): below = jnp.where(lat > 0, lax.ppermute(offsets, 'lat', up), none)]
    add x5 -> x0, other arithmetic: 13.3 us -> none  [the longest x4 10.6 us: local(): total[b] = total[b] + jnp.where(mask & here, values[p], 0.0)]
    another operation x5 -> x2, other arithmetic: 11.1 us -> 0.61 us  [the longest x1 0.6 us: local(): jnp.stack([offsets, above, below])]
    unnamed x17 -> x4, local copies, waits for them, and re-layouts: 3.25 us -> 0.01 us
    slice x3 -> x0, local copies, waits for them, and re-layouts: 2.75 us -> none  [the longest x1 1.45 us: local(): mask = row_mask(of[p, 0]) & exists]
    concatenate x1 -> x0, other arithmetic: 2.66 us -> none  [local(): return jnp.concatenate(total, axis=3)]
  transfers between devices with their start and end apart: 12 -> 2, of which waited for: 7 -> 0; matrix products, arithmetic and copies ran while one was open for 6% -> 4% of each run, Pallas kernels for 0% -> 0%
where the time goes in v2:
time: 146 us; the launch traced here: 145 us
  Pallas kernels  129 us (88%)
  starting transfers between devices  6.63 us (5%)
  between operations  4.01 us (3%)
  local copies, waits for them, and re-layouts  3.16 us (2%)
  other arithmetic  3.11 us (2%)
    pallas_call x1, Pallas kernels, local(): pl.pallas_call(functools.partial(wave_kernel, depth_count, lat_count), ou...  116 us
    pallas_call x1, Pallas kernels, local(): pl.pallas_call(deposit_kernel, grid=(slab,), out_shape=jax.ShapeDtypeStru...  8 us
    pallas_call x1, Pallas kernels, local(): pl.pallas_call(extract_kernel, grid=(slab,), out_shape=[pieces] * 3, in_s...  4.97 us
    ppermute x1, starting transfers between devices, local(): below = jnp.where(lat > 0, lax.ppermute(offsets, 'lat', up), none)  4.71 us
  transfers between devices with their start and end apart: 2, of which 0 were waited for; matrix products, arithmetic and copies ran while one was open for 4% of the time, Pallas kernels for 0%

profile of v2, /device:TPU:1, one launch (start us, length us, event | category | flops | bytes accessed | tf_op | source)
XLA Modules:
  0.0 145.5 jit_solution(14402046845729818353)
XLA Ops:
  0.0 0.0 copy-start.1
  0.0 0.0 copy-start
  0.0 4.7 %collective-permute-start = (s32[2,2]{1,0:T(2,128)}, s32[2,2]{1,0:T(2,128)S(1)}, u32[]{:S(2)}, u32[]{:S(2)}) collective-permute-start(s32[2,2]{1,0:T(2,128)} %param.11), channel_id=1, source_target_pairs={{0,1},{1,2},{2,3},{3,4},{4,5},{5,6},{6,7},{8,9},{9,10},{10,11},{11... | collective-permute-start | bytes 56 | tf_op jit(solution)/shard_map/ppermute | solution.py:320
  4.7 1.9 %collective-permute-start.1 = (s32[2,2]{1,0:T(2,128)}, s32[2,2]{1,0:T(2,128)S(1)}, u32[]{:S(2)}, u32[]{:S(2)}) collective-permute-start(s32[2,2]{1,0:T(2,128)} %param.11), channel_id=1, source_target_pairs={{1,0},{2,1},{3,2},{4,3},{5,4},{6,5},{7,6},{9,8},{10,9},{11,10},{12... | collective-permute-start | bytes 56 | tf_op jit(solution)/shard_map/ppermute | solution.py:321
  6.7 0.7 constant_dynamic-slice_fusion
  7.4 0.6 fusion.4
  11.9 1.9 %cosine_bitcast_fusion = (f32[1,256,256]{2,1,0:T(8,128)S(1)}, f32[1,256,256]{2,1,0:T(8,128)S(1)}) fusion(f32[256,256]{1,0:T(8,128)} %param.8), kind=kLoop, calls=%fused_computation.8 | loop fusion | bytes 786432 | tf_op jit(solution)/shard_map/stack | solution.py:314
  13.8 1.2 fusion.1
  15.0 1.3 fusion
  16.3 0.0 collective-permute-done
  16.3 0.0 collective-permute-done.1
  16.3 0.0 copy-done.1
  16.3 0.0 copy-done
  16.3 0.6 fusion.3
  16.9 5.0 %shard_map.73 = (f32[2,2,2,256,256]{4,3,2,1,0:T(8,128)}, f32[2,2,2,256,256]{4,3,2,1,0:T(8,128)}, f32[2,2,2,256,256]{4,3,2,1,0:T(8,128)}) custom-call(s32[1]{0:T(128)} %bitcast.place, s32[3,2,2]{2,1,0:T(2,128)} %get-tuple-element.19.offsets, f32[2,2,256,1024]{3,2,1,0:T(8,128)} %field.1), custom_call_target="tpu_custom_call" | custom-call | tf_op jit(solution)/shard_map/pallas_call | solution.py:329
  21.9 115.6 %shard_map.74 = (f32[2,2,2,256,256]{4,3,2,1,0:T(8,128)}, f32[2,2,2,256,256]{4,3,2,1,0:T(8,128)}, f32[2,2,2,256,256]{4,3,2,1,0:T(8,128)}) custom-call(f32[2,256,256]{2,1,0:T(8,128)} %get-tuple-element.25.probe, f32[2,256,256]{2,1,0:T(8,128)} %get-tuple-element.26.wave_table, bf16[2,3,256,256]{3,2,1,0:T(8,128)(2,1)} %constant.73.clone.tables, ...), custom_call_target="tpu_custom_call" | custom-call | tf_op jit(solution)/shard_map/pallas_call | solution.py:343
  137.5 8.0 %shard_map.75 = f32[2,2,256,1024]{3,2,1,0:T(8,128)} custom-call(s32[1]{0:T(128)} %bitcast.place, s32[3,2,2]{2,1,0:T(2,128)} %get-tuple-element.20.offsets, f32[2,2,2,256,256]{4,3,2,1,0:T(8,128)} %get-tuple-element.14.home, f32[2,2,2,256,256]{4,3,2,1,0:T(8,128)} %get-tuple-element.15.below, f32[2,2,2,256,256]{4,3,2,1,0:T(8,128)} %get-tuple-element.16.above), custom_call_target="tpu_custom_call" | custom-call | tf_op jit(solution)/shard_map/pallas_call | solution.py:362
  (1 shorter events, 0.0 us)
Async XLA Ops:
  0.0 16.3 %copy-start.1 = (s32[2]{0:T(128)S(1)}, s32[2]{0:T(128)}, u32[]{:S(2)}) copy-start(s32[2]{0:T(128)} %constant.74.clone) | copy-start | bytes 28
  0.0 16.3 %copy-start = (s32[2,2]{1,0:T(2,128)S(1)}, s32[2,2]{1,0:T(2,128)}, u32[]{:S(2)}) copy-start(s32[2,2]{1,0:T(2,128)} %param.11) | copy-start | bytes 52
  0.0 16.3 %collective-permute-start = (s32[2,2]{1,0:T(2,128)}, s32[2,2]{1,0:T(2,128)S(1)}, u32[]{:S(2)}, u32[]{:S(2)}) collective-permute-start(s32[2,2]{1,0:T(2,128)} %param.11), channel_id=1, source_target_pairs={{0,1},{1,2},{2,3},{3,4},{4,5},{5,6},{6,7},{8,9},{9,10},{10,11},{11... | collective-permute-start | bytes 56 | tf_op jit(solution)/shard_map/ppermute | solution.py:320
  4.7 11.6 %collective-permute-start.1 = (s32[2,2]{1,0:T(2,128)}, s32[2,2]{1,0:T(2,128)S(1)}, u32[]{:S(2)}, u32[]{:S(2)}) collective-permute-start(s32[2,2]{1,0:T(2,128)} %param.11), channel_id=1, source_target_pairs={{1,0},{2,1},{3,2},{4,3},{5,4},{6,5},{7,6},{9,8},{10,9},{11,10},{12... | collective-permute-start | bytes 56 | tf_op jit(solution)/shard_map/ppermute | solution.py:321

commit v3 on v2

--- a/solution.py
+++ b/solution.py
@@ -64,15 +64,41 @@
     return (rows >= start) & (rows < start + width)
 
 
-def extract_kernel(place, offsets, field, mine, to_up, to_down):
+def patch_corner(place, offsets, rank, p):
+    row, column = offsets[rank][p, 0], offsets[rank][p, 1]
+    if rank == 1:
+        row = jnp.where(place[0] > 0, row, place[2])
+    if rank == 2:
+        row = jnp.where(place[0] < place[1] - 1, row, place[2])
+    return row, column
+
+
+def extract_kernel(
+    place, own, below, above, probe, phase, field, mine, to_up, to_down, rolled, wave_table
+):
     width = field.shape[2]
     blocks = field.shape[3] // width
+    owned = mine.shape[0]
+    offsets = (own, below, above)
+
+    @pl.when(pl.program_id(0) == 0)
+    def _():
+        row, column = own[0, 0], own[0, 1]
+        for p in range(1, owned):
+            row = jnp.where(place[3] == p, own[p, 0], row)
+            column = jnp.where(place[3] == p, own[p, 1], column)
+        for c in range(2):
+            turned = pltpu.roll(probe[c], lax.rem(row, width), 0)
+            rolled[c] = pltpu.roll(turned, lax.rem(column, width), 1)
+        wave_table[0] = jnp.cos(phase[...])
+        wave_table[1] = jnp.sin(phase[...])
+
     lanes = lax.broadcasted_iota(jnp.int32, (width, width), 1)
-    for rank, out in enumerate((mine, to_up, to_down)):
-        for p in range(mine.shape[0]):
-            column = offsets[rank, p, 1]
+    for rank, out in ((0, mine), (2, to_up), (1, to_down)):
+        for p in range(owned):
+            row, column = patch_corner(place, offsets, rank, p)
             block = column // width
-            mask = row_mask(offsets[rank, p, 0], place[0], width)
+            mask = row_mask(row, place[0], width)
             first = mask & (lanes >= column - block * width)
             second = mask & (lanes < column - block * width)
             after = jnp.minimum(block + 1, blocks - 1)
@@ -82,24 +108,34 @@
                 out[p, 0, c] = jnp.where(first, a, jnp.where(second, b, 0.0))
 
 
-def deposit_kernel(place, offsets, home, below, above, out):
+def deposit_kernel(place, own, low_tile, high_tile, home, below, above, out):
     width = out.shape[2]
     blocks = out.shape[3] // width
-    lanes = lax.broadcasted_iota(jnp.int32, (width, width), 1)
-    for b in range(blocks):
-        for c in range(2):
-            total = jnp.zeros((width, width), jnp.float32)
-            for rank, terms in enumerate((home, below, above)):
-                for p in range(home.shape[0]):
-                    column = offsets[rank, p, 1]
-                    block = column // width
-                    rest = column - block * width
-                    low = jnp.where(block == b, rest, width)
-                    high = jnp.where(block + 1 == b, rest, 0)
-                    here = (lanes >= low) | (lanes < high)
-                    mask = row_mask(offsets[rank, p, 0], place[0], width) & here
-                    total += jnp.where(mask, terms[p, 0, c], 0.0)
-            out[c, 0, :, b * width : (b + 1) * width] = total
+    owned = home.shape[0]
+    strip = 32
+    lanes = lax.broadcasted_iota(jnp.int32, (strip, width), 1)
+    rows = lax.broadcasted_iota(jnp.int32, (strip, width), 0)
+    corners = []
+    for rank, terms in enumerate((home, below, above)):
+        for p in range(owned):
+            row, column = patch_corner(place, (own, low_tile, high_tile), rank, p)
+            corners.append((terms, p, row - place[0] * width, column // width, column))
+
+    @pl.loop(0, width // strip)
+    def _(i):
+        here_rows = pl.ds(pl.multiple_of(i * strip, strip), strip)
+        at = rows + i * strip
+        for b in range(blocks):
+            total = [jnp.zeros((strip, width), jnp.float32) for _ in range(2)]
+            for terms, p, start, block, column in corners:
+                rest = column - block * width
+                low = jnp.where(block == b, rest, width)
+                high = jnp.where(block + 1 == b, rest, 0)
+                mask = (at >= start) & (at < start + width) & ((lanes >= low) | (lanes < high))
+                for c in range(2):
+                    total[c] += jnp.where(mask, terms[p, 0, c, here_rows, :], 0.0)
+            for c in range(2):
+                out[c, 0, here_rows, b * width : (b + 1) * width] = total[c]
 
 
 def wave_kernel(
@@ -143,57 +179,69 @@
             device_id=device, device_id_type=pl.DeviceIdType.MESH,
         )
 
-    def upward(p, s):
-        return remote(to_up.at[p, s], from_below.at[p, s],
-                      z_send.at[0, p, s], z_recv.at[0, p, s], (depth, lat + 1))
-
-    def downward(p, s):
-        return remote(to_down.at[p, s], from_above.at[p, s],
-                      z_send.at[1, p, s], z_recv.at[1, p, s], (depth, lat - 1))
-
-    def inward(p, s):
+    def upward(p, s, c):
+        return remote(to_up.at[p, s, c], from_below.at[p, s, c],
+                      z_send.at[0, p, s, c], z_recv.at[0, p, s, c], (depth, lat + 1))
+
+    def downward(p, s, c):
+        return remote(to_down.at[p, s, c], from_above.at[p, s, c],
+                      z_send.at[1, p, s, c], z_recv.at[1, p, s, c], (depth, lat - 1))
+
+    def inward(p, s, c):
         place = depth * slab + s
-        return remote(merged.at[p, s], patches.at[place],
-                      in_send.at[p, s], in_recv.at[place], (owner(p), lat))
-
-    def outward(s):
+        return remote(merged.at[p, s, c], patches.at[place, c],
+                      in_send.at[p, s, c], in_recv.at[place, c], (owner(p), lat))
+
+    def outward(s, c):
         layer = lax.rem(s, slab)
         place = jnp.minimum(slot, owned - 1)
-        return remote(terms.at[s], home.at[place, layer],
-                      out_send.at[s], out_recv.at[place, layer], (s // slab, lat))
-
-    def back_up(p, s):
-        return remote(home.at[p, s], terms_below.at[p, s],
-                      back_send.at[0, p, s], back_recv.at[0, p, s], (depth, lat + 1))
-
-    def back_down(p, s):
-        return remote(home.at[p, s], terms_above.at[p, s],
-                      back_send.at[1, p, s], back_recv.at[1, p, s], (depth, lat - 1))
-
-    chunks = [(p, s) for s in range(slab) for p in range(owned)]
-    for p, s in chunks:
-        pl.when(has_above)(lambda: upward(p, s).start())
-        pl.when(has_below)(lambda: downward(p, s).start())
-    for p, s in chunks:
-        merged[p, s] = mine[p, s]
+        return remote(terms.at[s, c], home.at[place, layer, c],
+                      out_send.at[s, c], out_recv.at[place, layer, c], (s // slab, lat))
+
+    def back_up(p, s, c):
+        return remote(home.at[p, s, c], terms_below.at[p, s, c],
+                      back_send.at[0, p, s, c], back_recv.at[0, p, s, c], (depth, lat + 1))
+
+    def back_down(p, s, c):
+        return remote(home.at[p, s, c], terms_above.at[p, s, c],
+                      back_send.at[1, p, s, c], back_recv.at[1, p, s, c], (depth, lat - 1))
+
+    window = 2
+    chunks = [(p, s, c) for s in range(slab) for p in range(owned) for c in range(2)]
+
+    def start_pair(above, below, chunk):
+        pl.when(has_above)(lambda: above(*chunk).start())
+        pl.when(has_below)(lambda: below(*chunk).start())
+
+    def sent_pair(above, below, chunk):
+        pl.when(has_above)(lambda: above(*chunk).wait_send())
+        pl.when(has_below)(lambda: below(*chunk).wait_send())
+
+    for chunk in chunks[:window]:
+        start_pair(upward, downward, chunk)
+    for n, (p, s, c) in enumerate(chunks):
+        sent_pair(upward, downward, (p, s, c))
+        if n + window < len(chunks):
+            start_pair(upward, downward, chunks[n + window])
+        merged[p, s, c] = mine[p, s, c]
 
         @pl.when(has_below)
         def _():
-            upward(p, s).wait_recv()
-            merged[p, s] += from_below[p, s]
+            upward(p, s, c).wait_recv()
+            merged[p, s, c] += from_below[p, s, c]
 
         @pl.when(has_above)
         def _():
-            downward(p, s).wait_recv()
-            merged[p, s] += from_above[p, s]
+            downward(p, s, c).wait_recv()
+            merged[p, s, c] += from_above[p, s, c]
 
         @pl.when(owner(p) == depth)
         def _():
-            patches[depth * slab + s] = merged[p, s]
+            patches[depth * slab + s, c] = merged[p, s, c]
 
         @pl.when(owner(p) != depth)
         def _():
-            inward(p, s).start()
+            inward(p, s, c).start()
 
     @pl.when(active)
     def _():
@@ -207,8 +255,9 @@
 
             @pl.when(s // slab != depth)
             def _():
-                remote(merged.at[0, 0], patches.at[s], in_send.at[0, 0],
-                       in_recv.at[s], (depth, lat)).wait_recv()
+                for c in range(2):
+                    remote(merged.at[0, 0, c], patches.at[s, c], in_send.at[0, 0, c],
+                           in_recv.at[s, c], (depth, lat)).wait_recv()
 
             c, d = patches[s, 0], patches[s, 1]
             return c * a - d * b, c * b + d * a
@@ -247,7 +296,8 @@
 
             @pl.when(s // slab != depth)
             def _():
-                outward(s).start()
+                for c in range(2):
+                    outward(s, c).start()
 
             return a, b
 
@@ -260,38 +310,28 @@
 
         term(0)
 
-    back = [(p, s) for s in reversed(range(slab)) for p in range(owned)]
-    for p, s in back:
+    back = [(p, s, c) for s in reversed(range(slab)) for p in range(owned) for c in range(2)]
+    for n, (p, s, c) in enumerate(back):
 
         @pl.when(owner(p) == depth)
         def _():
-            home[p, s] = terms[depth * slab + s]
+            home[p, s, c] = terms[depth * slab + s, c]
 
         @pl.when(owner(p) != depth)
         def _():
-            remote(terms.at[0], home.at[p, s], out_send.at[0],
-                   out_recv.at[p, s], (depth, lat)).wait_recv()
-
-        pl.when(has_above)(lambda: back_up(p, s).start())
-        pl.when(has_below)(lambda: back_down(p, s).start())
-
-    for p, s in back:
-
-        @pl.when(has_below)
-        def _():
-            back_up(p, s).wait_recv()
-            downward(p, s).wait_send()
-            back_down(p, s).wait_send()
-
-        @pl.when(has_above)
-        def _():
-            back_down(p, s).wait_recv()
-            upward(p, s).wait_send()
-            back_up(p, s).wait_send()
-
-        @pl.when(owner(p) != depth)
-        def _():
-            inward(p, s).wait_send()
+            remote(terms.at[0, c], home.at[p, s, c], out_send.at[0, c],
+                   out_recv.at[p, s, c], (depth, lat)).wait_recv()
+
+        if n >= window:
+            sent_pair(back_up, back_down, back[n - window])
+        start_pair(back_up, back_down, (p, s, c))
+
+    for chunk in back[-window:]:
+        sent_pair(back_up, back_down, chunk)
+    for p, s, c in back:
+        pl.when(has_below)(lambda: back_up(p, s, c).wait_recv())
+        pl.when(has_above)(lambda: back_down(p, s, c).wait_recv())
+        pl.when(owner(p) != depth)(lambda: inward(p, s, c).wait_send())
 
     @pl.when(active)
     def _():
@@ -299,7 +339,8 @@
         def _(s):
             @pl.when(s // slab != depth)
             def _():
-                outward(s).wait_send()
+                for c in range(2):
+                    outward(s, c).wait_send()
 
 
 def local(probe, prop_phase, object_field, measured, offsets):
@@ -311,33 +352,32 @@
     depth = lax.axis_index("depth")
     lat = lax.axis_index("lat")
     tables = dft_tables(width)
-    wave_table = jnp.stack([jnp.cos(prop_phase), jnp.sin(prop_phase)])
 
     up = [(i, i + 1) for i in range(lat_count - 1)]
     down = [(i + 1, i) for i in range(lat_count - 1)]
-    far = -(lat_count + 2) * width
-    none = jnp.array([far, 0], jnp.int32) * jnp.ones((owned, 1), jnp.int32)
-    below = jnp.where(lat > 0, lax.ppermute(offsets, "lat", up), none)
-    above = jnp.where(lat < lat_count - 1, lax.ppermute(offsets, "lat", down), none)
-    place = lat.astype(jnp.int32)[None]
+    below = lax.ppermute(offsets, "lat", up)
+    above = lax.ppermute(offsets, "lat", down)
+    slot = (depth - lat * owned) % depth_count
+    place = jnp.stack(
+        [lat, jnp.int32(lat_count), jnp.int32(-(lat_count + 2) * width), slot]
+    ).astype(jnp.int32)
     smem = pl.BlockSpec(memory_space=pltpu.SMEM)
     vmem = pl.BlockSpec(memory_space=pltpu.VMEM)
     field_spec = pl.BlockSpec((2, 1, width, columns), lambda s: (0, s, 0, 0))
     piece_spec = pl.BlockSpec((owned, 1, 2, width, width), lambda s: (0, s, 0, 0, 0))
     pieces = jax.ShapeDtypeStruct((owned, slab, 2, width, width), jnp.float32)
     limit = 56 * 1024 * 1024
-    mine, to_up, to_down = pl.pallas_call(
+    whole = pl.BlockSpec(probe.shape, lambda s: (0, 0, 0))
+    mine, to_up, to_down, rolled, wave_table = pl.pallas_call(
         extract_kernel,
         grid=(slab,),
-        out_shape=[pieces] * 3,
-        in_specs=[smem, smem, field_spec],
-        out_specs=[piece_spec] * 3,
+        out_shape=[pieces] * 3 + [jax.ShapeDtypeStruct(probe.shape, jnp.float32)] * 2,
+        in_specs=[smem] * 4
+        + [whole, pl.BlockSpec(prop_phase.shape, lambda s: (0, 0)), field_spec],
+        out_specs=[piece_spec] * 3 + [whole] * 2,
         compiler_params=pltpu.CompilerParams(vmem_limit_bytes=limit),
-    )(place, jnp.stack([offsets, above, below]), object_field)
-
-    slot = (depth - lat * owned) % depth_count
-    offset = lax.dynamic_index_in_dim(offsets, jnp.minimum(slot, owned - 1), 0, keepdims=False)
-    rolled = jnp.roll(probe, (offset[0] % width, offset[1] % width), (1, 2))
+    )(place, offsets, below, above, probe, prop_phase, object_field)
+
     layers = (depth_count * slab, 2, width, width)
     dma = pltpu.SemaphoreType.DMA
     home, terms_below, terms_above = pl.pallas_call(
@@ -349,10 +389,10 @@
         + [pltpu.VMEM(layers, jnp.float32)] * 3
         + [
             pltpu.VMEM(layers[1:], jnp.float32),
-            dma((2, owned, slab)), dma((2, owned, slab)),
-            dma((owned, slab)), dma((layers[0],)),
-            dma((layers[0],)), dma((owned, slab)),
-            dma((2, owned, slab)), dma((2, owned, slab)),
+            dma((2, owned, slab, 2)), dma((2, owned, slab, 2)),
+            dma((owned, slab, 2)), dma((layers[0], 2)),
+            dma((layers[0], 2)), dma((owned, slab, 2)),
+            dma((2, owned, slab, 2)), dma((2, owned, slab, 2)),
         ],
         compiler_params=pltpu.CompilerParams(
             vmem_limit_bytes=limit, collective_id=0, has_side_effects=True
@@ -363,10 +403,10 @@
         deposit_kernel,
         grid=(slab,),
         out_shape=jax.ShapeDtypeStruct(object_field.shape, jnp.float32),
-        in_specs=[smem, smem] + [piece_spec] * 3,
+        in_specs=[smem] * 4 + [piece_spec] * 3,
         out_specs=field_spec,
         compiler_params=pltpu.CompilerParams(vmem_limit_bytes=limit),
-    )(place, jnp.stack([offsets, below, above]), home, terms_below, terms_above)
+    )(place, offsets, below, above, home, terms_below, terms_above)
 
 
 def solution(mesh):

time: 146 us -> 131 us (0.90)
  Pallas kernels: 129 us -> 123 us
  between operations: 4.01 us -> 0.05 us
  other arithmetic: 3.11 us -> 0.64 us
  local copies, waits for them, and re-layouts: 3.16 us -> 0.82 us
    pallas_call x1, Pallas kernels: 116 us -> 109 us  [local(): pl.pallas_call(functools.partial(wave_kernel, depth_count, lat_count), ou...]
    concatenate x2 -> x0, other arithmetic: 2.5 us -> none  [local(): rolled = jnp.roll(probe, (offset[0] % width, offset[1] % width), (1, 2))]
    pallas_call x1, Pallas kernels: 4.97 us -> 7.22 us  [local(): pl.pallas_call(extract_kernel, grid=(slab,), out_shape=[pieces] * 3 + [ja...]
    another operation x1 -> x0, local copies, waits for them, and re-layouts: 1.86 us -> none  [local(): wave_table = jnp.stack([jnp.cos(prop_phase), jnp.sin(prop_phase)])]
    pallas_call x1, Pallas kernels: 8 us -> 6.51 us  [local(): pl.pallas_call(deposit_kernel, grid=(slab,), out_shape=jax.ShapeDtypeStru...]
  transfers between devices with their start and end apart: 2 -> 2, of which waited for: 0 -> 1; matrix products, arithmetic and copies ran while one was open for 4% -> 0% of each run, Pallas kernels for 0% -> 0%
where the time goes in v3:
time: 131 us
  Pallas kernels  123 us (94%)
  starting transfers between devices  6.51 us (5%)
    pallas_call x1, Pallas kernels, local(): pl.pallas_call(functools.partial(wave_kernel, depth_count, lat_count), ou...  109 us
    pallas_call x1, Pallas kernels, local(): pl.pallas_call(extract_kernel, grid=(slab,), out_shape=[pieces] * 3 + [ja...  7.22 us
    pallas_call x1, Pallas kernels, local(): pl.pallas_call(deposit_kernel, grid=(slab,), out_shape=jax.ShapeDtypeStru...  6.51 us
    ppermute x1, starting transfers between devices, local(): below = lax.ppermute(offsets, 'lat', up)  4.55 us
  transfers between devices with their start and end apart: 2, of which 1 were waited for; matrix products, arithmetic and copies ran while one was open for 0% of the time, Pallas kernels for 0%

profile of v3, /device:TPU:1, one launch (start us, length us, event | category | flops | bytes accessed | tf_op | source)
XLA Modules:
  0.0 131.0 jit_solution(9854553820221856812)
XLA Ops:
  0.0 2.0 %collective-permute-start.1 = (s32[2,2]{1,0:T(2,128)}, s32[2,2]{1,0:T(2,128)S(1)}, u32[]{:S(2)}, u32[]{:S(2)}) collective-permute-start(s32[2,2]{1,0:T(2,128)} %own.3), channel_id=1, source_target_pairs={{1,0},{2,1},{3,2},{4,3},{5,4},{6,5},{7,6},{9,8},{10,9},{11,10},{12... | collective-permute-start | bytes 56 | tf_op jit(solution)/shard_map/ppermute | solution.py:359
  2.0 4.6 %collective-permute-start = (s32[2,2]{1,0:T(2,128)}, s32[2,2]{1,0:T(2,128)S(1)}, u32[]{:S(2)}, u32[]{:S(2)}) collective-permute-start(s32[2,2]{1,0:T(2,128)} %own.3), channel_id=1, source_target_pairs={{0,1},{1,2},{2,3},{3,4},{4,5},{5,6},{6,7},{8,9},{9,10},{10,11},{11... | collective-permute-start | bytes 56 | tf_op jit(solution)/shard_map/ppermute | solution.py:358
  6.5 0.6 pad_add_fusion.place
  7.2 0.0 collective-permute-done.1.above.high_tile
  7.2 0.0 copy-start
  7.2 0.2 collective-permute-done.below.low_tile
  7.4 0.3 copy-done
  7.7 0.0 copy-start.1
  7.7 0.5 copy-done.1
  8.3 7.2 %shard_map.64 = (f32[2,2,2,256,256]{4,3,2,1,0:T(8,128)}, f32[2,2,2,256,256]{4,3,2,1,0:T(8,128)}, f32[2,2,2,256,256]{4,3,2,1,0:T(8,128)}, f32[2,256,256]{2,1,0:T(8,128)}, f32[2,256,256]{2,1,0:T(8,128)}) custom-call(s32[4]{0:T(128)} %pad_add_fusion.place, s32[2,2]{1,0:T(2,128)} %own.3, s32[2,2]{1,0:T(2,128)} %copy-done.1, s32[2,2]{1,0:T(2,128)} %copy-done, ...), custom_call_target="tpu_custom_call" | custom-call | tf_op jit(solution)/shard_map/pallas_call | solution.py:371
  15.5 109.0 %shard_map.65 = (f32[2,2,2,256,256]{4,3,2,1,0:T(8,128)}, f32[2,2,2,256,256]{4,3,2,1,0:T(8,128)}, f32[2,2,2,256,256]{4,3,2,1,0:T(8,128)}) custom-call(f32[2,256,256]{2,1,0:T(8,128)} %get-tuple-element.13.probe, f32[2,256,256]{2,1,0:T(8,128)} %get-tuple-element.14.wave_table, bf16[2,3,256,256]{3,2,1,0:T(8,128)(2,1)} %constant.29.clone.tables, ...), custom_call_target="tpu_custom_call" | custom-call | tf_op jit(solution)/shard_map/pallas_call | solution.py:383
  124.5 6.5 %shard_map.66 = f32[2,2,256,1024]{3,2,1,0:T(8,128)} custom-call(s32[4]{0:T(128)} %pad_add_fusion.place, s32[2,2]{1,0:T(2,128)} %own.3, s32[2,2]{1,0:T(2,128)} %copy-done.1, s32[2,2]{1,0:T(2,128)} %copy-done, f32[2,2,2,256,256]{4,3,2,1,0:T(8,128)} %get-tuple-element.18.home, f32[2,2,2,256,256]{4,3,2,1,0:T(8,128)} %get-tuple-element.19.below, ...), custom_call_target="tpu_custom_call" | custom-call | tf_op jit(solution)/shard_map/pallas_call | solution.py:402
Async XLA Ops:
  0.0 7.2 %collective-permute-start.1 = (s32[2,2]{1,0:T(2,128)}, s32[2,2]{1,0:T(2,128)S(1)}, u32[]{:S(2)}, u32[]{:S(2)}) collective-permute-start(s32[2,2]{1,0:T(2,128)} %own.3), channel_id=1, source_target_pairs={{1,0},{2,1},{3,2},{4,3},{5,4},{6,5},{7,6},{9,8},{10,9},{11,10},{12... | collective-permute-start | bytes 56 | tf_op jit(solution)/shard_map/ppermute | solution.py:359
  2.0 5.5 %collective-permute-start = (s32[2,2]{1,0:T(2,128)}, s32[2,2]{1,0:T(2,128)S(1)}, u32[]{:S(2)}, u32[]{:S(2)}) collective-permute-start(s32[2,2]{1,0:T(2,128)} %own.3), channel_id=1, source_target_pairs={{0,1},{1,2},{2,3},{3,4},{4,5},{5,6},{6,7},{8,9},{9,10},{10,11},{11... | collective-permute-start | bytes 56 | tf_op jit(solution)/shard_map/ppermute | solution.py:358
  7.2 0.5 copy-start
  7.7 0.5 copy-start.1
